TPU v7x, 32 devices: a whole 2x2x4 slice. The times are simulated.
32 devices in a mesh: bx: 8 (over z, x), by: 4 (over y, core).
Axes of the slice: x: 2, y: 2, z: 4, core: 2. Of those that a mesh axis runs over, the one named last changes fastest.
Arguments:
- blocks: bfloat16 [8, 4, 32, 4096], P('bx', 'by'), as said below
- faces: bfloat16 [8, 4, 32, 4096], P('bx', 'by'), may hold values from -1.1953125 to 1.1953125
- tentative: bfloat16 [8, 4, 32, 4096], P('bx', 'by'), may hold values from -0.75 to 0.75
- aggregate: int32 [8, 4, 32], P('bx', 'by'), may hold values from 0 to 3
- ghost_labels: int32 [8, 4, 24], P('bx', 'by'), may hold values from 0 to 3, as said below
- rhs: float32 [8, 4, 6, 64, 32], P('bx', 'by'), may hold values from -6 to 6
- guess: float32 [8, 4, 6, 64, 32], P('bx', 'by'), may hold values from -6 to 6
- bounds: float32 [2], replicated, as said below
Outputs:
- smoothed: float32 [8, 4, 6, 64, 32], P('bx', 'by')
- coarse_local: float32 [8, 4, 256, 256], P('bx', 'by')
- coarse_ghost: float32 [8, 4, 4, 256, 256], P('bx', 'by')
Inputs may be any that keep to these rules, and one draw needn't show every extreme that they name: `ghost_labels`: each entry equals the aggregate number of the neighbouring brick's element across that face, 0 where the brick has no neighbour on that side. `blocks`: every diagonal entry of every block is at least 2. 0 < bounds[0] < bounds[1].
All inputs are finite; a program needn't handle non-finite values.
Results may differ from a plain program's by a relative error of at most 0.0029.
Values may be sent and summed in bfloat16 or wider, within the bound.
A program may use at most 64 MiB of HBM per device.

v0:
```python
import jax
import jax.numpy as jnp
from jax import lax
from jax.sharding import PartitionSpec as P

BLOCK = 64
NAGG = 4
EX = 4
EY = 8


def with_halo(block, sides, width):
    for axis, dim in sides:
        count = lax.axis_size(axis)
        forward = [(i, i + 1) for i in range(count - 1)]
        backward = [(target, source) for source, target in forward]
        low = lax.ppermute(
            lax.slice_in_dim(block, block.shape[dim] - width, None, axis=dim), axis, forward
        )
        high = lax.ppermute(lax.slice_in_dim(block, 0, width, axis=dim), axis, backward)
        block = jnp.concatenate([low, block, high], axis=dim)
    return block


def trace_blocks(prolong):
    dof_cube = prolong.reshape(EX, EY, 4, 4, 4, prolong.shape[-1])
    width = prolong.shape[-1]
    minus_x = dof_cube[:, :, 0].reshape(EX, EY, 16, width)
    plus_x = dof_cube[:, :, 3].reshape(EX, EY, 16, width)
    minus_y = dof_cube[:, :, :, 0].reshape(EX, EY, 16, width)
    plus_y = dof_cube[:, :, :, 3].reshape(EX, EY, 16, width)
    return (minus_x, plus_x, minus_y, plus_y)


def field_traces(vector_field):
    vectors = vector_field.shape[0]
    dof_cube = vector_field.reshape(vectors, 4, 4, 4, EX, EY)
    minus_x = dof_cube[:, 0].reshape(vectors, 16, EX, EY)
    plus_x = dof_cube[:, 3].reshape(vectors, 16, EX, EY)
    minus_y = dof_cube[:, :, 0].reshape(vectors, 16, EX, EY)
    plus_y = dof_cube[:, :, 3].reshape(vectors, 16, EX, EY)
    return (minus_x, plus_x, minus_y, plus_y)


def neighbour_rows(traces, edge_rows, axis_x, axis_y):
    minus_x, plus_x, minus_y, plus_y = traces
    low_x, high_x, low_y, high_y = edge_rows
    rows_x = plus_x.shape[axis_x]
    rows_y = plus_y.shape[axis_y]
    from_low_x = jnp.concatenate(
        [jnp.expand_dims(low_x, axis_x), lax.slice_in_dim(plus_x, 0, rows_x - 1, axis=axis_x)],
        axis_x,
    )
    from_high_x = jnp.concatenate(
        [lax.slice_in_dim(minus_x, 1, rows_x, axis=axis_x), jnp.expand_dims(high_x, axis_x)], axis_x
    )
    from_low_y = jnp.concatenate(
        [jnp.expand_dims(low_y, axis_y), lax.slice_in_dim(plus_y, 0, rows_y - 1, axis=axis_y)],
        axis_y,
    )
    from_high_y = jnp.concatenate(
        [lax.slice_in_dim(minus_y, 1, rows_y, axis=axis_y), jnp.expand_dims(high_y, axis_y)], axis_y
    )
    return jnp.stack([from_low_x, from_high_x, from_low_y, from_high_y])


def galerkin(diag_blocks, couplings, prolong, labels, traces, row_ghosts, label_ghosts):
    elements = EX * EY
    coarse = prolong.shape[-1]
    near_rows = neighbour_rows(traces, row_ghosts, 0, 1).reshape(4, elements, 16, coarse)
    grid_labels = labels.reshape(EX, EY)
    label_traces = (grid_labels, grid_labels, grid_labels, grid_labels)
    near_labels = neighbour_rows(label_traces, label_ghosts, 0, 1).reshape(4, elements)
    applied = jnp.einsum(
        "epq,eqr->epr", diag_blocks, prolong, preferred_element_type=jnp.float32
    ).astype(jnp.bfloat16)
    w_self = jnp.einsum("epa,epb->eab", prolong, applied, preferred_element_type=jnp.float32)
    coupled = jnp.einsum(
        "efpt,fetr->fepr", couplings, near_rows, preferred_element_type=jnp.float32
    ).astype(jnp.bfloat16)
    w_face = jnp.einsum("epa,fepb->feab", prolong, coupled, preferred_element_type=jnp.float32)
    numbers = jnp.arange(NAGG, dtype=jnp.int32)
    own_onehot = (labels[:, None] == numbers[None, :]).astype(jnp.float32)
    other_onehot = (near_labels[:, :, None] == numbers[None, None, :]).astype(jnp.float32)
    row_index = lax.broadcasted_iota(jnp.int32, (EX, EY), 0).reshape(elements)
    col_index = lax.broadcasted_iota(jnp.int32, (EX, EY), 1).reshape(elements)
    outside = jnp.stack(
        [row_index == 0, row_index == EX - 1, col_index == 0, col_index == EY - 1]
    ).astype(jnp.float32)
    pair_self = own_onehot[:, :, None] * own_onehot[:, None, :]
    pair_face = own_onehot[None, :, :, None] * other_onehot[:, :, None, :]
    local_part = jnp.einsum("eab,epr->apbr", pair_self, w_self, precision=lax.Precision.HIGHEST)
    local_part = local_part + jnp.einsum(
        "feab,fepr->apbr",
        pair_face * (1.0 - outside)[:, :, None, None],
        w_face,
        precision=lax.Precision.HIGHEST,
    )
    ghost_part = jnp.einsum(
        "feab,fepr->fapbr",
        pair_face * outside[:, :, None, None],
        w_face,
        precision=lax.Precision.HIGHEST,
    )
    coarse_width = NAGG * coarse
    return (
        local_part.reshape(coarse_width, coarse_width),
        ghost_part.reshape(4, coarse_width, coarse_width),
    )


def operate_brick(diag_wide, couple_wide, vector_field, traces, edge_rows):
    vectors = vector_field.shape[0]
    near_rows = neighbour_rows(traces, edge_rows, 2, 3).reshape(4, vectors, 16, EX * EY)
    own_term = jnp.einsum("epq,nqe->npe", diag_wide, vector_field, precision=lax.Precision.HIGHEST)
    face_term = jnp.einsum(
        "efpt,fnte->npe", couple_wide, near_rows, precision=lax.Precision.HIGHEST
    )
    return own_term + face_term


def chebyshev(operate, inverse, rhs_values, guess_values, bounds):
    lower_bound = bounds[0]
    upper_bound = bounds[1]
    centre = 0.5 * (upper_bound + lower_bound)
    half_width = 0.5 * (upper_bound - lower_bound)
    spread = centre / half_width
    factor = 1.0 / spread
    residue = rhs_values - operate(guess_values)
    update = inverse * residue / centre
    answer = guess_values + update
    for sweep_index in range(2):
        residue = residue - operate(update)
        next_factor = 1.0 / (2.0 * spread - factor)
        update = next_factor * factor * update + 2.0 * next_factor / half_width * inverse * residue
        answer = answer + update
        factor = next_factor
    return answer


def prolong_ghosts(prolong):
    coarse = prolong.shape[-1]
    extended = with_halo(prolong.reshape(EX, EY, BLOCK * coarse), (("bx", 0), ("by", 1)), 1)
    dof_cube = extended.reshape(EX + 2, EY + 2, 4, 4, 4, coarse)
    low_x = dof_cube[0, 1 : EY + 1, 3].reshape(EY, 16, coarse)
    high_x = dof_cube[EX + 1, 1 : EY + 1, 0].reshape(EY, 16, coarse)
    low_y = dof_cube[1 : EX + 1, 0, :, 3].reshape(EX, 16, coarse)
    high_y = dof_cube[1 : EX + 1, EY + 1, :, 0].reshape(EX, 16, coarse)
    return (low_x, high_x, low_y, high_y)


def field_edges(vector_field):
    vectors = vector_field.shape[0]
    traces = field_traces(vector_field)
    extended = with_halo(vector_field.reshape(vectors * BLOCK, EX, EY), (("bx", 1), ("by", 2)), 1)
    dof_cube = extended.reshape(vectors, 4, 4, 4, EX + 2, EY + 2)
    low_x = dof_cube[:, 3, :, :, 0, 1 : EY + 1].reshape(vectors, 16, EY)
    high_x = dof_cube[:, 0, :, :, EX + 1, 1 : EY + 1].reshape(vectors, 16, EY)
    low_y = dof_cube[:, :, 3, :, 1 : EX + 1, 0].reshape(vectors, 16, EX)
    high_y = dof_cube[:, :, 0, :, 1 : EX + 1, EY + 1].reshape(vectors, 16, EX)
    return (traces, (low_x, high_x, low_y, high_y))


def on_device(blocks, faces, tentative, aggregate, ghost_labels, rhs, guess, bounds):
    elements = EX * EY
    coarse = tentative.shape[-1] // BLOCK
    diag_blocks = blocks.reshape(elements, BLOCK, BLOCK)
    couplings = faces.reshape(elements, 4, BLOCK, 16)
    prolong = tentative.reshape(elements, BLOCK, coarse)
    labels = aggregate.reshape(elements)
    side_labels = ghost_labels.reshape(2 * EY + 2 * EX)
    label_ghosts = (
        side_labels[:EY],
        side_labels[EY : 2 * EY],
        side_labels[2 * EY : 2 * EY + EX],
        side_labels[2 * EY + EX :],
    )
    traces = trace_blocks(prolong)
    row_ghosts = prolong_ghosts(prolong)
    local_part, ghost_part = galerkin(
        diag_blocks, couplings, prolong, labels, traces, row_ghosts, label_ghosts
    )
    diag_wide = diag_blocks.astype(jnp.float32)
    couple_wide = couplings.astype(jnp.float32)

    def operate(vector_field):
        field_trace_set, edge_rows = field_edges(vector_field)
        return operate_brick(diag_wide, couple_wide, vector_field, field_trace_set, edge_rows)

    inverse = 1.0 / jnp.diagonal(diag_blocks, axis1=1, axis2=2).astype(jnp.float32).T
    vectors = rhs.shape[2]
    rhs_values = rhs.reshape(vectors, BLOCK, elements)
    guess_values = guess.reshape(vectors, BLOCK, elements)
    smoothed = chebyshev(operate, inverse, rhs_values, guess_values, bounds)
    return (smoothed[None, None], local_part[None, None], ghost_part[None, None])


def solution(mesh):
    placed = (
        P("bx", "by", None, None),
        P("bx", "by", None, None),
        P("bx", "by", None, None),
        P("bx", "by", None),
        P("bx", "by", None),
        P("bx", "by", None, None, None),
        P("bx", "by", None, None, None),
        P(),
    )
    return jax.shard_map(
        on_device,
        mesh=mesh,
        in_specs=placed,
        out_specs=(
            P("bx", "by", None, None, None),
            P("bx", "by", None, None),
            P("bx", "by", None, None, None),
        ),
        check_vma=False,
    )
```

profile of v0, /device:TPU:1, one launch (start us, length us, event | category | flops | bytes accessed | tf_op | source)
XLA Modules:
  0.0 163.8 jit_solution(5260862087785130566)
XLA Ops:
  2.3 4.5 %collective-permute-start = (f32[384,1,8]{0,2,1:T(8,128)}, f32[384,1,8]{0,2,1:T(8,128)}, u32[]{:S(2)}, u32[]{:S(2)}) collective-permute-start(f32[384,1,8]{0,2,1:T(8,128)} %get-tuple-element.70), channel_id=1, source_target_pairs={{0,4},{4,8},{8,12},{12,16},{16,20},{20,24},{24,28},{1,5},{5,9},{9,... | collective-permute-start | bytes 36872 | tf_op jit(solution)/shard_map/ppermute | solution.py:17
  9.6 4.6 %collective-permute-start.12 = (bf16[1,8,4096]{2,1,0:T(8,128)(2,1)}, bf16[1,8,4096]{2,1,0:T(8,128)(2,1)}, u32[]{:S(2)}, u32[]{:S(2)}) collective-permute-start(bf16[1,8,4096]{2,1,0:T(8,128)(2,1)} %get-tuple-element.57), channel_id=1, source_target_pairs={{0,4},{4,8},{8,12},{12,16},{16,20},{20,24},{24,28},{1,5},{5,9},{9,... | collective-permute-start | bytes 196616 | tf_op jit(solution)/shard_map/ppermute | solution.py:17
  32.4 4.5 %collective-permute-start.2 = (f32[384,6,1]{0,2,1:T(1,128)S(1)}, f32[384,6,1]{0,2,1:T(1,128)S(1)}, u32[]{:S(2)}, u32[]{:S(2)}) collective-permute-start(f32[384,6,1]{0,2,1:T(1,128)S(1)} %get-tuple-element.63), channel_id=1, source_target_pairs={{0,1},{1,2},{2,3},{4,5},{5,6},{6,7},{8,9},{9,10},{10,11},{12,13},{... | collective-permute-start | bytes 27656 | tf_op jit(solution)/shard_map/ppermute | solution.py:17
  37.0 1.9 %collective-permute-start.3 = (f32[384,6,1]{0,2,1:T(1,128)S(1)}, f32[384,6,1]{0,2,1:T(1,128)S(1)}, u32[]{:S(2)}, u32[]{:S(2)}) collective-permute-start(f32[384,6,1]{0,2,1:T(1,128)S(1)} %get-tuple-element.64), channel_id=1, source_target_pairs={{1,0},{2,1},{3,2},{5,4},{6,5},{7,6},{9,8},{10,9},{11,10},{13,12},{... | collective-permute-start | bytes 27656 | tf_op jit(solution)/shard_map/ppermute | solution.py:20
  45.3 2.1 %copy.394 = bf16[32,4,64,16]{2,3,1,0:T(8,128)(2,1)} copy(bf16[32,4,64,16]{0,3,2,1:T(8,128)(2,1)S(1)} %bitcast.217) | data formatting | bytes 524288 | tf_op jit(solution)/shard_map/reshape | solution.py:168
  57.6 1.6 multiply_divide_fusion
  59.4 4.3 %collective-permute-start.4 = (f32[384,1,8]{0,2,1:T(8,128)S(1)}, f32[384,1,8]{0,2,1:T(8,128)S(1)}, u32[]{:S(2)}, u32[]{:S(2)}) collective-permute-start(f32[384,1,8]{0,2,1:T(8,128)S(1)} %get-tuple-element.68), channel_id=1, source_target_pairs={{0,4},{4,8},{8,12},{12,16},{16,20},{20,24},{24,28},{1,5},{5,9},{9,... | collective-permute-start | bytes 36872 | tf_op jit(solution)/shard_map/ppermute | solution.py:17
  65.4 3.2 %collective-permute-done.5 = f32[384,1,8]{0,2,1:T(8,128)S(1)} collective-permute-done((f32[384,1,8]{0,2,1:T(8,128)S(1)}, f32[384,1,8]{0,2,1:T(8,128)S(1)}, u32[]{:S(2)}, u32[]{:S(2)}) %collective-permute-start.5) | collective-permute-done | bytes 12320 | tf_op jit(solution)/shard_map/ppermute | solution.py:20
  68.6 4.8 %collective-permute-start.6 = (f32[384,6,1]{0,2,1:T(1,128)S(1)}, f32[384,6,1]{0,2,1:T(1,128)S(1)}, u32[]{:S(2)}, u32[]{:S(2)}) collective-permute-start(f32[384,6,1]{0,2,1:T(1,128)S(1)} %get-tuple-element.61), channel_id=1, source_target_pairs={{0,1},{1,2},{2,3},{4,5},{5,6},{6,7},{8,9},{9,10},{10,11},{12,13},{... | collective-permute-start | bytes 27656 | tf_op jit(solution)/shard_map/ppermute | solution.py:17
  73.4 2.1 %collective-permute-start.7 = (f32[384,6,1]{0,2,1:T(1,128)S(1)}, f32[384,6,1]{0,2,1:T(1,128)S(1)}, u32[]{:S(2)}, u32[]{:S(2)}) collective-permute-start(f32[384,6,1]{0,2,1:T(1,128)S(1)} %get-tuple-element.62), channel_id=1, source_target_pairs={{1,0},{2,1},{3,2},{5,4},{6,5},{7,6},{9,8},{10,9},{11,10},{13,12},{... | collective-permute-start | bytes 27656 | tf_op jit(solution)/shard_map/ppermute | solution.py:20
  89.7 4.5 %collective-permute-start.8 = (f32[384,1,8]{0,2,1:T(8,128)S(1)}, f32[384,1,8]{0,2,1:T(8,128)S(1)}, u32[]{:S(2)}, u32[]{:S(2)}) collective-permute-start(f32[384,1,8]{0,2,1:T(8,128)S(1)} %get-tuple-element.66), channel_id=1, source_target_pairs={{0,4},{4,8},{8,12},{12,16},{16,20},{20,24},{24,28},{1,5},{5,9},{9,... | collective-permute-start | bytes 36872 | tf_op jit(solution)/shard_map/ppermute | solution.py:17
  96.0 2.7 %collective-permute-done.9 = f32[384,1,8]{0,2,1:T(8,128)S(1)} collective-permute-done((f32[384,1,8]{0,2,1:T(8,128)S(1)}, f32[384,1,8]{0,2,1:T(8,128)S(1)}, u32[]{:S(2)}, u32[]{:S(2)}) %collective-permute-start.9) | collective-permute-done | bytes 12320 | tf_op jit(solution)/shard_map/ppermute | solution.py:20
  98.7 4.6 %collective-permute-start.10 = (f32[384,6,1]{0,2,1:T(1,128)S(1)}, f32[384,6,1]{0,2,1:T(1,128)S(1)}, u32[]{:S(2)}, u32[]{:S(2)}) collective-permute-start(f32[384,6,1]{0,2,1:T(1,128)S(1)} %get-tuple-element.59), channel_id=1, source_target_pairs={{0,1},{1,2},{2,3},{4,5},{5,6},{6,7},{8,9},{9,10},{10,11},{12,13},{... | collective-permute-start | bytes 27656 | tf_op jit(solution)/shard_map/ppermute | solution.py:17
  103.3 1.9 %collective-permute-start.11 = (f32[384,6,1]{0,2,1:T(1,128)S(1)}, f32[384,6,1]{0,2,1:T(1,128)S(1)}, u32[]{:S(2)}, u32[]{:S(2)}) collective-permute-start(f32[384,6,1]{0,2,1:T(1,128)S(1)} %get-tuple-element.60), channel_id=1, source_target_pairs={{1,0},{2,1},{3,2},{5,4},{6,5},{7,6},{9,8},{10,9},{11,10},{13,12},{... | collective-permute-start | bytes 27656 | tf_op jit(solution)/shard_map/ppermute | solution.py:20
  119.9 3.0 %collective-permute-start.14 = (bf16[6,1,4096]{2,0,1:T(8,128)(2,1)S(1)}, bf16[6,1,4096]{2,0,1:T(8,128)(2,1)S(1)}, u32[]{:S(2)}, u32[]{:S(2)}) collective-permute-start(bf16[6,1,4096]{2,0,1:T(8,128)(2,1)S(1)} %get-tuple-element.55), channel_id=1, source_target_pairs={{0,1},{1,2},{2,3},{4,5},{5,6},{6,7},{8,9},{9,10},{10,11},{12,13},{... | collective-permute-start | bytes 147464 | tf_op jit(solution)/shard_map/ppermute | solution.py:17
  122.9 1.9 %collective-permute-start.15 = (bf16[6,1,4096]{2,0,1:T(8,128)(2,1)S(1)}, bf16[6,1,4096]{2,0,1:T(8,128)(2,1)S(1)}, u32[]{:S(2)}, u32[]{:S(2)}) collective-permute-start(bf16[6,1,4096]{2,0,1:T(8,128)(2,1)S(1)} %get-tuple-element.56), channel_id=1, source_target_pairs={{1,0},{2,1},{3,2},{5,4},{6,5},{7,6},{9,8},{10,9},{11,10},{13,12},{... | collective-permute-start | bytes 147464 | tf_op jit(solution)/shard_map/ppermute | solution.py:20
  126.4 2.0 %collective-permute-done.15 = bf16[6,1,4096]{2,0,1:T(8,128)(2,1)S(1)} collective-permute-done((bf16[6,1,4096]{2,0,1:T(8,128)(2,1)S(1)}, bf16[6,1,4096]{2,0,1:T(8,128)(2,1)S(1)}, u32[]{:S(2)}, u32[]{:S(2)}) %collective-permute-start.15) | collective-permute-done | bytes 49184 | tf_op jit(solution)/shard_map/ppermute | solution.py:20
  128.9 2.0 %reshape.294 = bf16[6,10,4,4,4,64]{5,4,3,2,0,1:T(4,128)(2,1)} reshape(bf16[6,10,4096]{2,0,1:T(8,128)(2,1)S(1)} %pad_maximum_fusion) | data formatting | bytes 983040 | tf_op jit(solution)/shard_map/reshape | solution.py:144
  132.7 3.3 %convolution_bitcast_fusion = f32[4,32,64,64,1]{2,3,0,1,4:T(8,128)} fusion(bf16[32,4,64,16]{2,3,1,0:T(8,128)(2,1)S(1)} %copy-done.3, bf16[1,32,16,64]{3,2,0,1:T(8,128)(2,1)S(1)} %bitcast.237, bf16[1,32,16,64]{3,2,0,1:T(8,128)(2,1)S(1)} %bitcast.236, bf16[1,32,16,64]{3,2,0,1:T(8,128)(2,1)S(1)} %bitcast.239, bf16[1,32,16,64]{3,2,0,1:T(8,128)(2,1)S(1)} %bitcast.238, ...), kind=kOutput, calls=%fused_computation.1 | convolution fusion | flops 84803584 | bytes 2883584 | tf_op jit(solution)/shard_map/epa,fepb->feab/dot_general | solution.py:81
  136.0 6.3 %copy.462 = f32[4,32,64,64,1]{3,1,0,4,2:T(8,128)} copy(f32[4,32,64,64,1]{2,3,0,1,4:T(8,128)} %convolution_bitcast_fusion) | data formatting | bytes 4194304 | tf_op jit(solution)/shard_map/epa,fepb->feab/transpose | solution.py:81
  142.2 6.2 %copy.464 = f32[4,32,64,64,1]{3,1,4,2,0:T(8,128)} copy(f32[4,32,64,64,1]{2,3,0,1,4:T(8,128)} %convolution_bitcast_fusion) | data formatting | bytes 4194304 | tf_op jit(solution)/shard_map/epa,fepb->feab/transpose | solution.py:81
  148.5 4.5 %convolution_bitcast_fusion.3 = f32[64,64,4,4]{1,3,2,0:T(4,128)S(1)} fusion(f32[4,32,64,64,1]{3,1,0,4,2:T(8,128)} %copy.462, f32[4,32]{1,0:T(4,128)S(1)} %broadcast_subtract_fusion, f32[4,32,4]{1,2,0:T(4,128)S(1)} %fusion.63, f32[32,4]{0,1:T(4,128)S(1)} %fusion.66), kind=kOutput, calls=%fused_computation.8 | convolution fusion | flops 100667392 | bytes 2362368 | tf_op jit(solution)/shard_map/feab,fepr->apbr/dot_general | solution.py:93
  155.2 5.9 %convolution_bitcast_fusion.1 = f32[4,4,64,4,64]{4,3,1,2,0:T(4,128)S(1)} fusion(f32[4,32,64,64,1]{3,1,4,2,0:T(8,128)} %copy.464, f32[4,32]{1,0:T(4,128)S(1)} %copy-done.27, f32[4,32,4]{1,2,0:T(4,128)S(1)} %fusion.63, f32[32,4]{0,1:T(4,128)S(1)} %fusion.66), kind=kOutput, calls=%fused_computation.5 | convolution fusion | flops 100667392 | bytes 3148800 | tf_op jit(solution)/shard_map/feab,fepr->fapbr/dot_general | solution.py:99
  161.7 2.1 %broadcast_in_dim_reshape.9 = f32[1,1,4,256,256]{4,3,2,1,0:T(8,128)} reshape(f32[4,4,64,4,64]{4,3,2,1,0:T(4,128)S(1)} %copy.454) | data formatting | bytes 2097152 | tf_op jit(solution)/shard_map/broadcast_in_dim;reshape | solution.py:195
  (248 shorter events, 74.5 us)
Async XLA Ops:
  2.3 28.7 %collective-permute-start = (f32[384,1,8]{0,2,1:T(8,128)}, f32[384,1,8]{0,2,1:T(8,128)}, u32[]{:S(2)}, u32[]{:S(2)}) collective-permute-start(f32[384,1,8]{0,2,1:T(8,128)} %get-tuple-element.70), channel_id=1, source_target_pairs={{0,4},{4,8},{8,12},{12,16},{16,20},{20,24},{24,28},{1,5},{5,9},{9,... | collective-permute-start | bytes 36872 | tf_op jit(solution)/shard_map/ppermute | solution.py:17
  6.8 24.9 %collective-permute-start.1 = (f32[384,1,8]{0,2,1:T(8,128)}, f32[384,1,8]{0,2,1:T(8,128)}, u32[]{:S(2)}, u32[]{:S(2)}) collective-permute-start(f32[384,1,8]{0,2,1:T(8,128)} %get-tuple-element.69), channel_id=1, source_target_pairs={{4,0},{8,4},{12,8},{16,12},{20,16},{24,20},{28,24},{5,1},{9,5},{13... | collective-permute-start | bytes 36872 | tf_op jit(solution)/shard_map/ppermute | solution.py:20
  9.6 108.2 %collective-permute-start.12 = (bf16[1,8,4096]{2,1,0:T(8,128)(2,1)}, bf16[1,8,4096]{2,1,0:T(8,128)(2,1)}, u32[]{:S(2)}, u32[]{:S(2)}) collective-permute-start(bf16[1,8,4096]{2,1,0:T(8,128)(2,1)} %get-tuple-element.57), channel_id=1, source_target_pairs={{0,4},{4,8},{8,12},{12,16},{16,20},{20,24},{24,28},{1,5},{5,9},{9,... | collective-permute-start | bytes 196616 | tf_op jit(solution)/shard_map/ppermute | solution.py:17
  14.2 104.6 %collective-permute-start.13 = (bf16[1,8,4096]{2,1,0:T(8,128)(2,1)}, bf16[1,8,4096]{2,1,0:T(8,128)(2,1)}, u32[]{:S(2)}, u32[]{:S(2)}) collective-permute-start(bf16[1,8,4096]{2,1,0:T(8,128)(2,1)} %get-tuple-element.58), channel_id=1, source_target_pairs={{4,0},{8,4},{12,8},{16,12},{20,16},{24,20},{28,24},{5,1},{9,5},{13... | collective-permute-start | bytes 196616 | tf_op jit(solution)/shard_map/ppermute | solution.py:20
  29.8 11.1 %copy-start.6 = (f32[6,4,1,4,4,8]{5,4,3,2,1,0:T(4,128)S(1)}, f32[6,4,1,4,4,8]{5,4,3,2,1,0:T(4,128)}, u32[]{:S(2)}) copy-start(f32[6,4,1,4,4,8]{5,4,3,2,1,0:T(4,128)} %get-tuple-element.50) | copy-start | bytes 36868
  32.4 10.8 %copy-start.21 = (f32[384,6,8]{0,2,1:T(8,128)}, f32[384,6,8]{0,2,1:T(8,128)S(1)}, u32[]{:S(2)}) copy-start(f32[384,6,8]{0,2,1:T(8,128)S(1)} %constant_dynamic-update-slice_fusion) | copy-start | bytes 221188
  32.4 17.5 %collective-permute-start.2 = (f32[384,6,1]{0,2,1:T(1,128)S(1)}, f32[384,6,1]{0,2,1:T(1,128)S(1)}, u32[]{:S(2)}, u32[]{:S(2)}) collective-permute-start(f32[384,6,1]{0,2,1:T(1,128)S(1)} %get-tuple-element.63), channel_id=1, source_target_pairs={{0,1},{1,2},{2,3},{4,5},{5,6},{6,7},{8,9},{9,10},{10,11},{12,13},{... | collective-permute-start | bytes 27656 | tf_op jit(solution)/shard_map/ppermute | solution.py:17
  37.0 13.0 %collective-permute-start.3 = (f32[384,6,1]{0,2,1:T(1,128)S(1)}, f32[384,6,1]{0,2,1:T(1,128)S(1)}, u32[]{:S(2)}, u32[]{:S(2)}) collective-permute-start(f32[384,6,1]{0,2,1:T(1,128)S(1)} %get-tuple-element.64), channel_id=1, source_target_pairs={{1,0},{2,1},{3,2},{5,4},{6,5},{7,6},{9,8},{10,9},{11,10},{13,12},{... | collective-permute-start | bytes 27656 | tf_op jit(solution)/shard_map/ppermute | solution.py:20
  59.4 6.0 %collective-permute-start.4 = (f32[384,1,8]{0,2,1:T(8,128)S(1)}, f32[384,1,8]{0,2,1:T(8,128)S(1)}, u32[]{:S(2)}, u32[]{:S(2)}) collective-permute-start(f32[384,1,8]{0,2,1:T(8,128)S(1)} %get-tuple-element.68), channel_id=1, source_target_pairs={{0,4},{4,8},{8,12},{12,16},{16,20},{20,24},{24,28},{1,5},{5,9},{9,... | collective-permute-start | bytes 36872 | tf_op jit(solution)/shard_map/ppermute | solution.py:17
  63.7 4.9 %collective-permute-start.5 = (f32[384,1,8]{0,2,1:T(8,128)S(1)}, f32[384,1,8]{0,2,1:T(8,128)S(1)}, u32[]{:S(2)}, u32[]{:S(2)}) collective-permute-start(f32[384,1,8]{0,2,1:T(8,128)S(1)} %get-tuple-element.67), channel_id=1, source_target_pairs={{4,0},{8,4},{12,8},{16,12},{20,16},{24,20},{28,24},{5,1},{9,5},{13... | collective-permute-start | bytes 36872 | tf_op jit(solution)/shard_map/ppermute | solution.py:20
  68.6 9.3 %collective-permute-start.6 = (f32[384,6,1]{0,2,1:T(1,128)S(1)}, f32[384,6,1]{0,2,1:T(1,128)S(1)}, u32[]{:S(2)}, u32[]{:S(2)}) collective-permute-start(f32[384,6,1]{0,2,1:T(1,128)S(1)} %get-tuple-element.61), channel_id=1, source_target_pairs={{0,1},{1,2},{2,3},{4,5},{5,6},{6,7},{8,9},{9,10},{10,11},{12,13},{... | collective-permute-start | bytes 27656 | tf_op jit(solution)/shard_map/ppermute | solution.py:17
  73.4 5.0 %collective-permute-start.7 = (f32[384,6,1]{0,2,1:T(1,128)S(1)}, f32[384,6,1]{0,2,1:T(1,128)S(1)}, u32[]{:S(2)}, u32[]{:S(2)}) collective-permute-start(f32[384,6,1]{0,2,1:T(1,128)S(1)} %get-tuple-element.62), channel_id=1, source_target_pairs={{1,0},{2,1},{3,2},{5,4},{6,5},{7,6},{9,8},{10,9},{11,10},{13,12},{... | collective-permute-start | bytes 27656 | tf_op jit(solution)/shard_map/ppermute | solution.py:20
  89.7 6.2 %collective-permute-start.8 = (f32[384,1,8]{0,2,1:T(8,128)S(1)}, f32[384,1,8]{0,2,1:T(8,128)S(1)}, u32[]{:S(2)}, u32[]{:S(2)}) collective-permute-start(f32[384,1,8]{0,2,1:T(8,128)S(1)} %get-tuple-element.66), channel_id=1, source_target_pairs={{0,4},{4,8},{8,12},{12,16},{16,20},{20,24},{24,28},{1,5},{5,9},{9,... | collective-permute-start | bytes 36872 | tf_op jit(solution)/shard_map/ppermute | solution.py:17
  94.2 4.4 %collective-permute-start.9 = (f32[384,1,8]{0,2,1:T(8,128)S(1)}, f32[384,1,8]{0,2,1:T(8,128)S(1)}, u32[]{:S(2)}, u32[]{:S(2)}) collective-permute-start(f32[384,1,8]{0,2,1:T(8,128)S(1)} %get-tuple-element.65), channel_id=1, source_target_pairs={{4,0},{8,4},{12,8},{16,12},{20,16},{24,20},{28,24},{5,1},{9,5},{13... | collective-permute-start | bytes 36872 | tf_op jit(solution)/shard_map/ppermute | solution.py:20
  98.7 8.9 %collective-permute-start.10 = (f32[384,6,1]{0,2,1:T(1,128)S(1)}, f32[384,6,1]{0,2,1:T(1,128)S(1)}, u32[]{:S(2)}, u32[]{:S(2)}) collective-permute-start(f32[384,6,1]{0,2,1:T(1,128)S(1)} %get-tuple-element.59), channel_id=1, source_target_pairs={{0,1},{1,2},{2,3},{4,5},{5,6},{6,7},{8,9},{9,10},{10,11},{12,13},{... | collective-permute-start | bytes 27656 | tf_op jit(solution)/shard_map/ppermute | solution.py:17
  103.3 5.0 %collective-permute-start.11 = (f32[384,6,1]{0,2,1:T(1,128)S(1)}, f32[384,6,1]{0,2,1:T(1,128)S(1)}, u32[]{:S(2)}, u32[]{:S(2)}) collective-permute-start(f32[384,6,1]{0,2,1:T(1,128)S(1)} %get-tuple-element.60), channel_id=1, source_target_pairs={{1,0},{2,1},{3,2},{5,4},{6,5},{7,6},{9,8},{10,9},{11,10},{13,12},{... | collective-permute-start | bytes 27656 | tf_op jit(solution)/shard_map/ppermute | solution.py:20
  116.1 8.7 %copy-start.24 = (f32[6,64,32]{1,0,2:T(8,128)S(1)}, f32[6,64,32]{1,0,2:T(8,128)}, u32[]{:S(2)}) copy-start(f32[6,64,32]{1,0,2:T(8,128)} %get-tuple-element.83) | copy-start | bytes 147460
  116.1 8.7 %copy-start.25 = (f32[64,32]{0,1:T(8,128)S(1)}, f32[64,32]{0,1:T(8,128)}, u32[]{:S(2)}) copy-start(f32[64,32]{0,1:T(8,128)} %get-tuple-element.71) | copy-start | bytes 24580
  116.3 8.5 %copy-start.30 = (f32[6,64,32]{1,0,2:T(8,128)S(1)}, f32[6,64,32]{1,0,2:T(8,128)}, u32[]{:S(2)}) copy-start(f32[6,64,32]{1,0,2:T(8,128)} %get-tuple-element.85) | copy-start | bytes 147460
  119.9 6.6 %collective-permute-start.14 = (bf16[6,1,4096]{2,0,1:T(8,128)(2,1)S(1)}, bf16[6,1,4096]{2,0,1:T(8,128)(2,1)S(1)}, u32[]{:S(2)}, u32[]{:S(2)}) collective-permute-start(bf16[6,1,4096]{2,0,1:T(8,128)(2,1)S(1)} %get-tuple-element.55), channel_id=1, source_target_pairs={{0,1},{1,2},{2,3},{4,5},{5,6},{6,7},{8,9},{9,10},{10,11},{12,13},{... | collective-permute-start | bytes 147464 | tf_op jit(solution)/shard_map/ppermute | solution.py:17
  122.9 5.6 %collective-permute-start.15 = (bf16[6,1,4096]{2,0,1:T(8,128)(2,1)S(1)}, bf16[6,1,4096]{2,0,1:T(8,128)(2,1)S(1)}, u32[]{:S(2)}, u32[]{:S(2)}) collective-permute-start(bf16[6,1,4096]{2,0,1:T(8,128)(2,1)S(1)} %get-tuple-element.56), channel_id=1, source_target_pairs={{1,0},{2,1},{3,2},{5,4},{6,5},{7,6},{9,8},{10,9},{11,10},{13,12},{... | collective-permute-start | bytes 147464 | tf_op jit(solution)/shard_map/ppermute | solution.py:20
  126.4 6.0 %copy-start.13 = (bf16[4,7,16,64]{3,2,1,0:T(8,128)(2,1)S(1)}, bf16[4,7,16,64]{3,2,1,0:T(8,128)(2,1)}, u32[]{:S(2)}) copy-start(bf16[4,7,16,64]{3,2,1,0:T(8,128)(2,1)} %slice.376) | copy-start | bytes 172036
  128.9 3.7 %copy-start.14 = (bf16[3,8,1,4,4,64]{5,4,3,2,1,0:T(4,128)(2,1)S(1)}, bf16[3,8,1,4,4,64]{5,4,3,2,1,0:T(4,128)(2,1)}, u32[]{:S(2)}) copy-start(bf16[3,8,1,4,4,64]{5,4,3,2,1,0:T(4,128)(2,1)} %get-tuple-element.52) | copy-start | bytes 147460
  128.9 3.7 %copy-start.4 = (bf16[32,64,64,1]{2,1,0,3:T(8,128)(2,1)S(1)}, bf16[32,64,64,1]{2,1,0,3:T(8,128)(2,1)}, u32[]{:S(2)}) copy-start(bf16[32,64,64,1]{2,1,0,3:T(8,128)(2,1)} %reshape.306) | copy-start | bytes 786436
  (23 other events, 59.9 us)
where the time goes:
time: 165 us; the launch traced here: 164 us
  local copies, waits for them, and re-layouts  66.9 us (41%)
  starting transfers between devices  47.9 us (29%)
  matrix products  23.9 us (14%)
  other arithmetic  11.4 us (7%)
  waiting for transfers between devices  9.05 us (5%)
  between operations  4.64 us (3%)
    ppermute x8, starting transfers between devices, with_halo(): lax.ppermute(lax.slice_in_dim(block, block.shape[dim] - width, None, axis...  34.9 us
    ppermute x8, starting transfers between devices, with_halo(): lax.ppermute(lax.slice_in_dim(block, 0, width, axis=dim), axis, backward)  13 us
    transpose x2, local copies, waits for them, and re-layouts, galerkin(): jnp.einsum('epa,fepb->feab', prolong, coupled, preferred_element_type=jnp...  12.5 us
    ppermute x8, waiting for transfers between devices, with_halo(): lax.ppermute(lax.slice_in_dim(block, 0, width, axis=dim), axis, backward)  9.03 us
    unnamed x74, local copies, waits for them, and re-layouts  5.96 us
    dot_general x1, matrix products, galerkin(): jnp.einsum('feab,fepr->fapbr', pair_face * outside[:, :, None, None], w_f...  5.89 us
    dot_general x3, matrix products, operate_brick(): jnp.einsum('efpt,fnte->npe', couple_wide, near_rows, precision=lax.Precis...  4.54 us
    dot_general x1, matrix products, galerkin(): jnp.einsum('feab,fepr->apbr', pair_face * (1.0 - outside)[:, :, None, Non...  4.54 us
  transfers between devices with their start and end apart: 16, of which 5 were waited for; matrix products, arithmetic and copies ran while one was open for 39% of the time, Pallas kernels for 0%

commit v1 on v0

v1 whole, which is shorter than its diff:
```python
import jax
import jax.numpy as jnp
from jax import lax
from jax.experimental import pallas as pl
from jax.experimental.pallas import tpu as pltpu
from jax.sharding import PartitionSpec as P

BLOCK = 64
NAGG = 4
EX = 4
EY = 8
E = EX * EY
F32 = jnp.float32
BF16 = jnp.bfloat16
NT = (((1,), (1,)), ((), ()))


def trace_source(column):
    face = column >> 4
    t = column & 15
    spread = ((t >> 2) << 4) + (t & 3)
    return jnp.where(
        face == 0, 48 + t, jnp.where(face == 1, t, jnp.where(face == 2, spread + 12, spread))
    )


def kernel(
    nx,
    ny,
    bounds,
    labels,
    ghost_labels,
    m_ref,
    t_ref,
    rhs_ref,
    guess_ref,
    out_ref,
    local_ref,
    ghost_ref,
    gbuf,
    hx,
    hy,
    tg,
    thx,
    thy,
    tat,
    xh,
    xl,
    xg,
    obuf,
    send_sem,
    recv_sem,
):
    bx = lax.axis_index("bx")
    by = lax.axis_index("by")
    has_from = (bx > 0, bx < nx - 1, by > 0, by < ny - 1)
    has_to = (bx < nx - 1, bx > 0, by < ny - 1, by > 0)
    target = ({"bx": bx + 1}, {"bx": bx - 1}, {"by": by + 1}, {"by": by - 1})
    count = sum(flag.astype(jnp.int32) for flag in has_from)
    barrier = pltpu.get_barrier_semaphore()
    for f in range(4):

        @pl.when(has_to[f])
        def _(f=f):
            pl.semaphore_signal(
                barrier, inc=1, device_id=target[f], device_id_type=pl.DeviceIdType.MESH
            )

    def field_copy(r, f):
        if f < 2:
            src, dst = gbuf.at[r, EX - 1 if f == 0 else 0], hx.at[r, f]
        else:
            src, dst = gbuf.at[r, :, EY - 1 if f == 2 else 0], hy.at[r, f - 2]
        return pltpu.make_async_remote_copy(
            src_ref=src,
            dst_ref=dst,
            send_sem=send_sem.at[r, f],
            recv_sem=recv_sem.at[r, f],
            device_id=target[f],
            device_id_type=pl.DeviceIdType.MESH,
        )

    def tent_copy(f):
        rows = pl.ds(16 * f, 16)
        if f < 2:
            src, dst = tg.at[EX - 1 if f == 0 else 0, :, rows], thx.at[f]
        else:
            src, dst = tg.at[:, EY - 1 if f == 2 else 0, rows], thy.at[f - 2]
        return pltpu.make_async_remote_copy(
            src_ref=src,
            dst_ref=dst,
            send_sem=send_sem.at[3, f],
            recv_sem=recv_sem.at[3, f],
            device_id=target[f],
            device_id_type=pl.DeviceIdType.MESH,
        )

    def start(make):
        for f in range(4):

            @pl.when(has_to[f])
            def _(f=f):
                make(f).start()

    def wait_recv(make):
        for f in range(4):

            @pl.when(has_from[f])
            def _(f=f):
                make(f).wait_recv()

    def wait_send(make):
        for f in range(4):

            @pl.when(has_to[f])
            def _(f=f):
                make(f).wait_send()

    row = lax.broadcasted_iota(jnp.int32, (128, 128), 0)
    col = lax.broadcasted_iota(jnp.int32, (128, 128), 1)
    gather = jnp.where(
        (col >= BLOCK) & (row == trace_source(col - BLOCK)), 1.0, 0.0
    ).astype(BF16)
    lane = lax.broadcasted_iota(jnp.int32, (1, 1, 1, 128), 3)

    def split(values):
        high = values.astype(BF16)
        low = (values - high.astype(F32)).astype(BF16)
        return high, low

    def send_traces(r, field):
        high, low = split(field.reshape(E * 8, 128))
        both = jnp.dot(
            jnp.concatenate([high, low], axis=0), gather, preferred_element_type=F32
        )
        gbuf[r] = (both[: E * 8] + both[E * 8 :]).reshape(EX, EY, 8, 128)
        if r == 0:
            pl.semaphore_wait(barrier, count)
        start(lambda f: field_copy(r, f))

    def operate(r, field):
        wait_recv(lambda f: field_copy(r, f))
        own = gbuf[r]
        from0 = jnp.concatenate([hx[r, 0][None], own[:-1]], axis=0)
        from1 = jnp.concatenate([own[1:], hx[r, 1][None]], axis=0)
        from2 = jnp.concatenate([hy[r, 0][:, None], own[:, :-1]], axis=1)
        from3 = jnp.concatenate([own[:, 1:], hy[r, 1][:, None]], axis=1)
        near = jnp.where(
            lane < 80, from0, jnp.where(lane < 96, from1, jnp.where(lane < 112, from2, from3))
        )
        full = field + near.reshape(E, 8, 128)
        high, low = split(full)
        for e in range(E):
            both = lax.dot_general(
                jnp.concatenate([high[e], low[e]], axis=0),
                m_ref[e],
                NT,
                preferred_element_type=F32,
            )
            obuf[e, :, :BLOCK] = both[:8] + both[8:]
        return obuf[...]

    guess = guess_ref[...]
    obuf[...] = jnp.zeros_like(obuf)
    for f in range(4):

        @pl.when(jnp.logical_not(has_from[f]))
        def _(f=f):
            if f < 2:
                hx[:, f] = jnp.zeros((3, EY, 8, 128), F32)
                thx[f] = jnp.zeros((EY, 16, 128), BF16)
            else:
                hy[:, f - 2] = jnp.zeros((3, EX, 8, 128), F32)
                thy[f - 2] = jnp.zeros((EX, 16, 128), BF16)

    send_traces(0, guess)

    row = lax.broadcasted_iota(jnp.int32, (BLOCK, BLOCK), 0)
    col = lax.broadcasted_iota(jnp.int32, (BLOCK, BLOCK), 1)
    pick = jnp.where(col == trace_source(row), 1.0, 0.0).astype(BF16)
    for e in range(E):
        tg[e // EY, e % EY] = jnp.dot(pick, t_ref[e], preferred_element_type=F32).astype(BF16)
    start(tent_copy)

    low_b = jnp.full((1, 1, 128), bounds[0], F32)
    high_b = jnp.full((1, 1, 128), bounds[1], F32)
    centre = 0.5 * (high_b + low_b)
    half_width = 0.5 * (high_b - low_b)
    spread = centre / half_width
    eye = jnp.where(
        lax.broadcasted_iota(jnp.int32, (BLOCK, 128), 0)
        == lax.broadcasted_iota(jnp.int32, (BLOCK, 128), 1),
        1.0,
        0.0,
    )
    diagonal = jnp.stack(
        [jnp.sum(m_ref[e].astype(F32) * eye, axis=0, keepdims=True) for e in range(E)]
    )
    lane3 = lax.broadcasted_iota(jnp.int32, (1, 1, 128), 2)
    inverse = jnp.where(lane3 < BLOCK, 1.0 / jnp.where(lane3 < BLOCK, diagonal, 1.0), 0.0)

    group = lax.broadcasted_iota(jnp.int32, (1, 256), 1) >> 6

    def mask(label):
        return jnp.where(group == label, 1.0, 0.0).astype(BF16)

    def wide(half):
        return jnp.concatenate([half, half], axis=1)

    zero16 = jnp.zeros((16, 256), BF16)

    def products(e):
        ix, iy = e // EY, e % EY
        own = wide(t_ref[e]) * mask(labels[e])
        near = [zero16] * 4
        for f, (jx, jy) in enumerate(((ix - 1, iy), (ix + 1, iy), (ix, iy - 1), (ix, iy + 1))):
            if 0 <= jx < EX and 0 <= jy < EY:
                near[f] = wide(tg[jx, jy, 16 * f : 16 * f + 16]) * mask(labels[jx * EY + jy])
        stacked = jnp.concatenate([own] + near, axis=0)
        x = jnp.dot(m_ref[e], stacked, preferred_element_type=F32)
        high, low = split(x)
        xh[BLOCK * e : BLOCK * (e + 1)] = high
        xl[BLOCK * e : BLOCK * (e + 1)] = low

    for e in range(E):
        products(e)

    residue = rhs_ref[...] - operate(0, guess)
    update = inverse * residue / centre
    send_traces(1, update)
    answer = guess + update
    factor = 1.0 / spread

    eye_b = eye.astype(BF16)
    lane2 = lax.broadcasted_iota(jnp.int32, (1, 128), 1)
    for j in range(E // 2):
        pair = t_ref[2 * j : 2 * j + 2].reshape(128, 128)
        turned = lax.dot_general(eye_b, pair, NT, preferred_element_type=F32)
        number = jnp.where(lane2 < BLOCK, labels[2 * j], labels[2 * j + 1])
        for a in range(NAGG):
            tat[BLOCK * a : BLOCK * (a + 1), 128 * j : 128 * (j + 1)] = jnp.where(
                number == a, turned, 0.0
            ).astype(BF16)
    local_ref[...] = jnp.dot(tat[...], xh[...], preferred_element_type=F32) + jnp.dot(
        tat[...], xl[...], preferred_element_type=F32
    )

    def step(r, residue, update, factor):
        residue = residue - operate(r, update)
        after = 1.0 / (2.0 * spread - factor)
        update = after * factor * update + (2.0 * after / half_width) * inverse * residue
        return residue, update, after

    residue, update, factor = step(1, residue, update, factor)
    send_traces(2, update)
    answer = answer + update

    wait_recv(tent_copy)
    zero64 = jnp.zeros((BLOCK, 256), BF16)

    def ghost_product(f, e, rows, label):
        near = [zero16] * 4
        near[f] = wide(rows) * mask(label)
        stacked = jnp.concatenate([zero64] + near, axis=0)
        return jnp.dot(m_ref[e], stacked, preferred_element_type=F32).astype(BF16)

    for f in range(2):
        for iy in range(EY):
            e = (0 if f == 0 else EX - 1) * EY + iy
            xg[f, BLOCK * iy : BLOCK * (iy + 1)] = ghost_product(
                f, e, thx[f, iy], ghost_labels[f * EY + iy]
            )
        first = 0 if f == 0 else (EX - 1) * EY * BLOCK
        ghost_ref[f] = jnp.dot(
            tat[:, first : first + EY * BLOCK], xg[f], preferred_element_type=F32
        )
    for f in range(2, 4):
        total = None
        for ix in range(EX):
            e = ix * EY + (0 if f == 2 else EY - 1)
            x = ghost_product(f, e, thy[f - 2, ix], ghost_labels[2 * EY + (f - 2) * EX + ix])
            parts = [x, zero64] if f == 2 else [zero64, x]
            xg[f, 128 * ix : 128 * (ix + 1)] = jnp.concatenate(parts, axis=0)
            first = 128 * (e // 2)
            part = jnp.dot(
                tat[:, first : first + 128],
                xg[f, 128 * ix : 128 * (ix + 1)],
                preferred_element_type=F32,
            )
            total = part if total is None else total + part
        ghost_ref[f] = total

    residue, update, factor = step(2, residue, update, factor)
    out_ref[...] = answer + update
    for r in range(3):
        wait_send(lambda f: field_copy(r, f))
    wait_send(tent_copy)


def on_device(nx, ny, blocks, faces, tentative, aggregate, ghost_labels, rhs, guess, bounds):
    diag = blocks.reshape(E, BLOCK, BLOCK)
    couple = faces.reshape(E, 4, BLOCK, 16).transpose(0, 2, 1, 3).reshape(E, BLOCK, BLOCK)
    matrix = jnp.concatenate([diag, couple], axis=-1)
    prolong = tentative.reshape(E, BLOCK, BLOCK)
    twice = jnp.concatenate([prolong, prolong], axis=-1)
    vectors = rhs.shape[2]

    def by_element(field):
        moved = field.reshape(vectors, BLOCK, E).transpose(2, 0, 1)
        return jnp.pad(moved, ((0, 0), (0, 8 - vectors), (0, 128 - BLOCK)))

    vmem = pl.BlockSpec(memory_space=pltpu.VMEM)
    smem = pl.BlockSpec(memory_space=pltpu.SMEM)
    smoothed, local, ghost = pl.pallas_call(
        lambda *refs: kernel(nx, ny, *refs),
        out_shape=(
            jax.ShapeDtypeStruct((E, 8, 128), F32),
            jax.ShapeDtypeStruct((256, 256), F32),
            jax.ShapeDtypeStruct((4, 256, 256), F32),
        ),
        in_specs=[smem] * 3 + [vmem] * 4,
        out_specs=(vmem, vmem, vmem),
        scratch_shapes=[
            pltpu.VMEM((3, EX, EY, 8, 128), F32),
            pltpu.VMEM((3, 2, EY, 8, 128), F32),
            pltpu.VMEM((3, 2, EX, 8, 128), F32),
            pltpu.VMEM((EX, EY, BLOCK, 128), BF16),
            pltpu.VMEM((2, EY, 16, 128), BF16),
            pltpu.VMEM((2, EX, 16, 128), BF16),
            pltpu.VMEM((256, E * BLOCK), BF16),
            pltpu.VMEM((E * BLOCK, 256), BF16),
            pltpu.VMEM((E * BLOCK, 256), BF16),
            pltpu.VMEM((4, 512, 256), BF16),
            pltpu.VMEM((E, 8, 128), F32),
            pltpu.SemaphoreType.DMA((4, 4)),
            pltpu.SemaphoreType.DMA((4, 4)),
        ],
        compiler_params=pltpu.CompilerParams(
            collective_id=0, has_side_effects=True, vmem_limit_bytes=32 * 1024 * 1024
        ),
        name="galerkin_smooth",
    )(
        bounds,
        aggregate.reshape(E),
        ghost_labels.reshape(2 * EY + 2 * EX),
        matrix,
        twice,
        by_element(rhs),
        by_element(guess),
    )
    smoothed = smoothed[:, :vectors, :BLOCK].transpose(1, 2, 0)
    return (smoothed[None, None], local[None, None], ghost[None, None])


def solution(mesh):
    nx, ny = mesh.shape["bx"], mesh.shape["by"]
    placed = (
        P("bx", "by", None, None),
        P("bx", "by", None, None),
        P("bx", "by", None, None),
        P("bx", "by", None),
        P("bx", "by", None),
        P("bx", "by", None, None, None),
        P("bx", "by", None, None, None),
        P(),
    )
    return jax.shard_map(
        lambda *args: on_device(nx, ny, *args),
        mesh=mesh,
        in_specs=placed,
        out_specs=(
            P("bx", "by", None, None, None),
            P("bx", "by", None, None),
            P("bx", "by", None, None, None),
        ),
        check_vma=False,
    )
```

time: 165 us -> 28.2 us (0.17)
  the two profiles are of different devices: /device:TPU:1 before, /device:TPU:0 now
where the time goes in v1:
time: 28.2 us; the launch traced here: 27.9 us
  Pallas kernels  17.1 us (61%)
  local copies, waits for them, and re-layouts  9.51 us (34%)
  between operations  0.76 us (3%)
  other arithmetic  0.58 us (2%)
    pallas_call x1, Pallas kernels, on_device(): pl.pallas_call(lambda *refs: kernel(nx, ny, *refs), out_shape=(jax.ShapeD...  17.1 us
    unnamed x20, local copies, waits for them, and re-layouts  6.78 us
    transpose x1, local copies, waits for them, and re-layouts, on_device(): faces.reshape(E, 4, BLOCK, 16).transpose(0, 2, 1, 3)  1.35 us
    concatenate x1, other arithmetic, on_device(): matrix = jnp.concatenate([diag, couple], axis=-1)  0.58 us

profile of v1, /device:TPU:0, one launch (start us, length us, event | category | flops | bytes accessed | tf_op | source)
XLA Modules:
  0.0 27.9 jit_solution(13705600556691300266)
XLA Ops:
  0.6 1.4 %copy.15 = bf16[1,1,32,4096]{2,3,1,0:T(8,128)(2,1)S(1)} copy(bf16[1,1,32,4096]{3,2,1,0:T(8,128)(2,1)} %param.9) | data formatting | bytes 524288 | tf_op args[1]
  2.1 1.3 %copy.16 = bf16[32,64,4,16]{1,3,2,0:T(8,128)(2,1)S(1)} copy(bf16[32,64,4,16]{0,3,1,2:T(8,128)(2,1)S(1)} %bitcast.30) | data formatting | bytes 524288 | tf_op jit(solution)/shard_map/transpose | solution.py:302
  3.4 0.0 copy-start.3
  3.4 0.3 copy.17
  3.7 0.7 %copy-done.3 = bf16[1,1,32,4096]{3,2,1,0:T(8,128)(2,1)S(1)} copy-done((bf16[1,1,32,4096]{3,2,1,0:T(8,128)(2,1)S(1)}, bf16[1,1,32,4096]{3,2,1,0:T(8,128)(2,1)}, u32[]{:S(2)}) %copy-start.3) | copy-done | bytes 262168
  4.4 0.5 %reshape.32 = bf16[32,64,64]{2,1,0:T(8,128)(2,1)S(1)} reshape(bf16[1,1,32,4096]{3,2,1,0:T(8,128)(2,1)S(1)} %copy-done.3) | data formatting | bytes 524288 | tf_op jit(solution)/shard_map/reshape | solution.py:301
  4.9 0.4 %copy-done.4 = bf16[1,1,32,4096]{3,2,1,0:T(8,128)(2,1)S(1)} copy-done((bf16[1,1,32,4096]{3,2,1,0:T(8,128)(2,1)S(1)}, bf16[1,1,32,4096]{3,2,1,0:T(8,128)(2,1)}, u32[]{:S(2)}) %copy-start.4) | copy-done | bytes 262168
  5.3 0.5 %reshape.35 = bf16[32,64,64]{2,1,0:T(8,128)(2,1)S(1)} reshape(bf16[1,1,32,4096]{3,2,1,0:T(8,128)(2,1)S(1)} %copy-done.4) | data formatting | bytes 524288 | tf_op jit(solution)/shard_map/reshape | solution.py:304
  5.9 0.0 copy-start.5
  5.9 0.6 %pad_maximum_fusion = (bf16[32,64,128]{2,1,0:T(8,128)(2,1)S(1)}, bf16[32,64,128]{2,1,0:T(8,128)(2,1)S(1)}) fusion(bf16[32,64,64]{2,1,0:T(8,128)(2,1)S(1)} %copy.17, bf16[32,64,64]{2,1,0:T(8,128)(2,1)S(1)} %reshape.32, bf16[32,64,64]{2,1,0:T(8,128)(2,1)S(1)} %reshape.35), kind=kLoop, calls=%fused_computation | loop fusion | flops 2097152 | bytes 1835008 | tf_op jit(solution)/shard_map/concatenate | solution.py:303
  6.5 0.3 %copy-done.5 = f32[1,1,6,64,32]{3,4,2,1,0:T(8,128)S(1)} copy-done((f32[1,1,6,64,32]{3,4,2,1,0:T(8,128)S(1)}, f32[1,1,6,64,32]{3,4,2,1,0:T(8,128)}, u32[]{:S(2)}) %copy-start.5) | copy-done | bytes 49176
  6.8 0.1 copy.24
  6.8 0.0 copy-start.6
  6.9 0.9 %copy-done.6 = f32[1,1,6,64,32]{3,4,2,1,0:T(8,128)S(1)} copy-done((f32[1,1,6,64,32]{3,4,2,1,0:T(8,128)S(1)}, f32[1,1,6,64,32]{3,4,2,1,0:T(8,128)}, u32[]{:S(2)}) %copy-start.6) | copy-done | bytes 49176
  7.7 0.1 copy.23
  7.8 0.0 copy-start
  7.8 0.0 copy-start.2
  7.8 0.6 %copy-done = f32[2]{0:T(128)S(1)} copy-done((f32[2]{0:T(128)S(1)}, f32[2]{0:T(128)}, u32[]{:S(2)}) %copy-start) | copy-done | bytes 32
  8.5 0.0 copy-done.1
  8.5 0.0 copy-done.2
  8.5 17.1 %galerkin_smooth.1 = (f32[32,8,128]{2,1,0:T(8,128)S(1)}, f32[256,256]{1,0:T(8,128)S(1)}, f32[4,256,256]{2,1,0:T(8,128)S(1)}) custom-call(f32[2]{0:T(128)S(1)} %copy-done, s32[32]{0:T(128)S(1)} %bitcast.28, s32[24]{0:T(128)S(1)} %bitcast.29, bf16[32,64,128]{2,1,0:T(8,128)(2,1)S(1)} %get-tuple-element.15.refs_3_, ...), custom_call_target="tpu_custom_call" | custom-call | tf_op jit(solution)/shard_map/galerkin_smooth/pallas_call | solution.py:314
  25.6 0.7 %copy.20 = f32[1,1,6,64,32]{3,4,2,1,0:T(8,128)} copy(f32[1,1,6,64,32]{3,2,4,1,0:T(8,128)S(1)} %slice_bitcast_fusion) | data formatting | bytes 98304
  26.3 0.7 %copy.27 = f32[1,1,256,256]{3,2,1,0:T(8,128)} copy(f32[1,1,256,256]{3,2,1,0:T(8,128)S(1)} %bitcast.27) | data formatting | bytes 524288
  27.0 1.0 %copy.28 = f32[1,1,4,256,256]{4,3,2,1,0:T(8,128)} copy(f32[1,1,4,256,256]{4,3,2,1,0:T(8,128)S(1)} %bitcast.26) | data formatting | bytes 2097152
  (5 shorter events, 0.0 us)
Async XLA Ops:
  3.4 1.0 %copy-start.3 = (bf16[1,1,32,4096]{3,2,1,0:T(8,128)(2,1)S(1)}, bf16[1,1,32,4096]{3,2,1,0:T(8,128)(2,1)}, u32[]{:S(2)}) copy-start(bf16[1,1,32,4096]{3,2,1,0:T(8,128)(2,1)} %param.8) | copy-start | bytes 786436
  4.4 0.9 %copy-start.4 = (bf16[1,1,32,4096]{3,2,1,0:T(8,128)(2,1)S(1)}, bf16[1,1,32,4096]{3,2,1,0:T(8,128)(2,1)}, u32[]{:S(2)}) copy-start(bf16[1,1,32,4096]{3,2,1,0:T(8,128)(2,1)} %param.10) | copy-start | bytes 786436
  5.9 0.9 %copy-start.5 = (f32[1,1,6,64,32]{3,4,2,1,0:T(8,128)S(1)}, f32[1,1,6,64,32]{3,4,2,1,0:T(8,128)}, u32[]{:S(2)}) copy-start(f32[1,1,6,64,32]{3,4,2,1,0:T(8,128)} %param.13) | copy-start | bytes 147460
  6.8 0.9 %copy-start.6 = (f32[1,1,6,64,32]{3,4,2,1,0:T(8,128)S(1)}, f32[1,1,6,64,32]{3,4,2,1,0:T(8,128)}, u32[]{:S(2)}) copy-start(f32[1,1,6,64,32]{3,4,2,1,0:T(8,128)} %param.14) | copy-start | bytes 147460
  7.8 0.7 %copy-start = (f32[2]{0:T(128)S(1)}, f32[2]{0:T(128)}, u32[]{:S(2)}) copy-start(f32[2]{0:T(128)} %refs_0_.1) | copy-start | bytes 28
  7.8 0.7 %copy-start.1 = (s32[1,1,32]{2,1,0:T(1,128)S(1)}, s32[1,1,32]{2,1,0:T(1,128)}, u32[]{:S(2)}) copy-start(s32[1,1,32]{2,1,0:T(1,128)} %param.11) | copy-start | bytes 388
  7.8 0.7 %copy-start.2 = (s32[1,1,24]{2,1,0:T(1,128)S(1)}, s32[1,1,24]{2,1,0:T(1,128)}, u32[]{:S(2)}) copy-start(s32[1,1,24]{2,1,0:T(1,128)} %param.12) | copy-start | bytes 292

commit v2 on v1

--- a/solution.py
+++ b/solution.py
@@ -12,6 +12,7 @@
 E = EX * EY
 F32 = jnp.float32
 BF16 = jnp.bfloat16
+VMEM_LIMIT = 60 * 1024 * 1024
 NT = (((1,), (1,)), ((), ()))
 
 
@@ -30,13 +31,28 @@
     bounds,
     labels,
     ghost_labels,
-    m_ref,
-    t_ref,
-    rhs_ref,
-    guess_ref,
+    blocks_hbm,
+    faces_hbm,
+    tent_hbm,
+    rhs_hbm,
+    guess_hbm,
+    out_hbm,
+    local_hbm,
+    ghost_hbm,
     out_ref,
     local_ref,
     ghost_ref,
+    blocks_in,
+    faces_in,
+    tent_in,
+    rhs_in,
+    guess_in,
+    rhs_ref,
+    guess_ref,
+    rows32,
+    trows32,
+    m_ref,
+    t_ref,
     gbuf,
     hx,
     hy,
@@ -48,9 +64,32 @@
     xl,
     xg,
     obuf,
+    load_sem,
+    store_sem,
     send_sem,
     recv_sem,
 ):
+    loads = [
+        pltpu.make_async_copy(src, dst, load_sem.at[i])
+        for i, (src, dst) in enumerate(
+            (
+                (guess_hbm, guess_in),
+                (tent_hbm, tent_in),
+                (faces_hbm, faces_in),
+                (blocks_hbm, blocks_in),
+                (rhs_hbm, rhs_in),
+            )
+        )
+    ]
+    for load in loads:
+        load.start()
+    stores = [
+        pltpu.make_async_copy(src, dst, store_sem.at[i])
+        for i, (src, dst) in enumerate(
+            [(ghost_ref.at[f], ghost_hbm.at[f]) for f in range(4)]
+            + [(local_ref, local_hbm), (out_ref, out_hbm)]
+        )
+    ]
     bx = lax.axis_index("bx")
     by = lax.axis_index("by")
     has_from = (bx > 0, bx < nx - 1, by > 0, by < ny - 1)
@@ -160,7 +199,16 @@
             obuf[e, :, :BLOCK] = both[:8] + both[8:]
         return obuf[...]
 
-    guess = guess_ref[...]
+    vectors = guess_in.shape[0]
+
+    def by_element(source, target):
+        target[...] = jnp.zeros_like(target)
+        for n in range(vectors):
+            target[pl.ds(n, E, stride=8), :] = jnp.concatenate(
+                [source[n], jnp.zeros((E, BLOCK), F32)], axis=1
+            )
+        return target[...].reshape(E, 8, 128)
+
     obuf[...] = jnp.zeros_like(obuf)
     for f in range(4):
 
@@ -173,7 +221,22 @@
                 hy[:, f - 2] = jnp.zeros((3, EX, 8, 128), F32)
                 thy[f - 2] = jnp.zeros((EX, 16, 128), BF16)
 
+    loads[0].wait()
+    guess = by_element(guess_in, guess_ref)
     send_traces(0, guess)
+
+    left = lax.broadcasted_iota(jnp.int32, (E, 128), 1) < BLOCK
+
+    def turn(values):
+        return pltpu.roll(values, BLOCK, 1)
+
+    loads[1].wait()
+    for c in range(E):
+        even = tent_in[:, 128 * c : 128 * (c + 1)].astype(F32)
+        odd = turn(even)
+        trows32[pl.ds(2 * c, E, stride=BLOCK), :] = jnp.where(left, even, odd)
+        trows32[pl.ds(2 * c + 1, E, stride=BLOCK), :] = jnp.where(left, odd, even)
+    t_ref[...] = trows32[...].reshape(E, BLOCK, 128).astype(BF16)
 
     row = lax.broadcasted_iota(jnp.int32, (BLOCK, BLOCK), 0)
     col = lax.broadcasted_iota(jnp.int32, (BLOCK, BLOCK), 1)
@@ -181,6 +244,30 @@
     for e in range(E):
         tg[e // EY, e % EY] = jnp.dot(pick, t_ref[e], preferred_element_type=F32).astype(BF16)
     start(tent_copy)
+
+    row = lax.broadcasted_iota(jnp.int32, (512, 512), 0)
+    col = lax.broadcasted_iota(jnp.int32, (512, 512), 1)
+    source = (((col >> 4) & 3) << 7) + ((col >> 6) << 4) + (col & 15)
+    order = jnp.where(row == source, 1.0, 0.0).astype(BF16)
+    loads[2].wait()
+    grouped = jnp.concatenate(
+        [
+            jnp.concatenate(
+                [faces_in[:, 1024 * f + 128 * h : 1024 * f + 128 * (h + 1)] for f in range(4)],
+                axis=1,
+            )
+            for h in range(8)
+        ],
+        axis=0,
+    )
+    couple = jnp.dot(grouped, order, preferred_element_type=F32)
+    loads[3].wait()
+    for c in range(E):
+        own = blocks_in[:, 128 * c : 128 * (c + 1)].astype(F32)
+        side = couple[E * (c // 4) : E * (c // 4 + 1), 128 * (c % 4) : 128 * (c % 4 + 1)]
+        rows32[pl.ds(2 * c, E, stride=BLOCK), :] = jnp.where(left, own, turn(side))
+        rows32[pl.ds(2 * c + 1, E, stride=BLOCK), :] = jnp.where(left, turn(own), side)
+    m_ref[...] = rows32[...].reshape(E, BLOCK, 128).astype(BF16)
 
     low_b = jnp.full((1, 1, 128), bounds[0], F32)
     high_b = jnp.full((1, 1, 128), bounds[1], F32)
@@ -194,7 +281,10 @@
         0.0,
     )
     diagonal = jnp.stack(
-        [jnp.sum(m_ref[e].astype(F32) * eye, axis=0, keepdims=True) for e in range(E)]
+        [
+            jnp.sum(rows32[BLOCK * e : BLOCK * (e + 1)] * eye, axis=0, keepdims=True)
+            for e in range(E)
+        ]
     )
     lane3 = lax.broadcasted_iota(jnp.int32, (1, 1, 128), 2)
     inverse = jnp.where(lane3 < BLOCK, 1.0 / jnp.where(lane3 < BLOCK, diagonal, 1.0), 0.0)
@@ -222,14 +312,16 @@
         xh[BLOCK * e : BLOCK * (e + 1)] = high
         xl[BLOCK * e : BLOCK * (e + 1)] = low
 
-    for e in range(E):
-        products(e)
-
-    residue = rhs_ref[...] - operate(0, guess)
+    loads[4].wait()
+    rhs = by_element(rhs_in, rhs_ref)
+    residue = rhs - operate(0, guess)
     update = inverse * residue / centre
     send_traces(1, update)
     answer = guess + update
     factor = 1.0 / spread
+
+    for e in range(E):
+        products(e)
 
     eye_b = eye.astype(BF16)
     lane2 = lax.broadcasted_iota(jnp.int32, (1, 128), 1)
@@ -241,10 +333,6 @@
             tat[BLOCK * a : BLOCK * (a + 1), 128 * j : 128 * (j + 1)] = jnp.where(
                 number == a, turned, 0.0
             ).astype(BF16)
-    local_ref[...] = jnp.dot(tat[...], xh[...], preferred_element_type=F32) + jnp.dot(
-        tat[...], xl[...], preferred_element_type=F32
-    )
-
     def step(r, residue, update, factor):
         residue = residue - operate(r, update)
         after = 1.0 / (2.0 * spread - factor)
@@ -255,6 +343,12 @@
     send_traces(2, update)
     answer = answer + update
 
+    local_ref[...] = jnp.dot(tat[...], xh[...], preferred_element_type=F32) + jnp.dot(
+        tat[...], xl[...], preferred_element_type=F32
+    )
+
+    stores[4].start()
+
     wait_recv(tent_copy)
     zero64 = jnp.zeros((BLOCK, 256), BF16)
 
@@ -274,6 +368,7 @@
         ghost_ref[f] = jnp.dot(
             tat[:, first : first + EY * BLOCK], xg[f], preferred_element_type=F32
         )
+        stores[f].start()
     for f in range(2, 4):
         total = None
         for ix in range(EX):
@@ -289,38 +384,65 @@
             )
             total = part if total is None else total + part
         ghost_ref[f] = total
+        stores[f].start()
 
     residue, update, factor = step(2, residue, update, factor)
-    out_ref[...] = answer + update
+    guess_ref[...] = (answer + update).reshape(E * 8, 128)
+    for n in range(vectors):
+        out_ref[n] = guess_ref[pl.ds(n, E, stride=8), :][:, :BLOCK]
+    stores[5].start()
+    for store in stores:
+        store.wait()
     for r in range(3):
         wait_send(lambda f: field_copy(r, f))
     wait_send(tent_copy)
 
 
+def store_kernel(smoothed, local, ghost, smoothed_out, local_out, ghost_out, sem):
+    pairs = [(ghost.at[f], ghost_out.at[f]) for f in range(4)]
+    pairs += [(local, local_out), (smoothed, smoothed_out)]
+    copies = [
+        pltpu.make_async_copy(src, dst, sem.at[i]) for i, (src, dst) in enumerate(pairs)
+    ]
+    for copy in copies:
+        copy.start()
+    for copy in copies:
+        copy.wait()
+
+
 def on_device(nx, ny, blocks, faces, tentative, aggregate, ghost_labels, rhs, guess, bounds):
-    diag = blocks.reshape(E, BLOCK, BLOCK)
-    couple = faces.reshape(E, 4, BLOCK, 16).transpose(0, 2, 1, 3).reshape(E, BLOCK, BLOCK)
-    matrix = jnp.concatenate([diag, couple], axis=-1)
-    prolong = tentative.reshape(E, BLOCK, BLOCK)
-    twice = jnp.concatenate([prolong, prolong], axis=-1)
     vectors = rhs.shape[2]
 
-    def by_element(field):
-        moved = field.reshape(vectors, BLOCK, E).transpose(2, 0, 1)
-        return jnp.pad(moved, ((0, 0), (0, 8 - vectors), (0, 128 - BLOCK)))
-
-    vmem = pl.BlockSpec(memory_space=pltpu.VMEM)
+    def values_last(field):
+        return field.reshape(vectors, BLOCK, E).transpose(0, 2, 1)
+
     smem = pl.BlockSpec(memory_space=pltpu.SMEM)
+    hbm = pl.BlockSpec(memory_space=pltpu.HBM)
+    shapes = (
+        jax.ShapeDtypeStruct((vectors, E, BLOCK), F32),
+        jax.ShapeDtypeStruct((256, 256), F32),
+        jax.ShapeDtypeStruct((4, 256, 256), F32),
+    )
     smoothed, local, ghost = pl.pallas_call(
         lambda *refs: kernel(nx, ny, *refs),
-        out_shape=(
-            jax.ShapeDtypeStruct((E, 8, 128), F32),
-            jax.ShapeDtypeStruct((256, 256), F32),
-            jax.ShapeDtypeStruct((4, 256, 256), F32),
-        ),
-        in_specs=[smem] * 3 + [vmem] * 4,
-        out_specs=(vmem, vmem, vmem),
+        out_shape=shapes,
+        in_specs=[smem] * 3 + [hbm] * 5,
+        out_specs=(hbm, hbm, hbm),
         scratch_shapes=[
+            pltpu.VMEM((vectors, E, BLOCK), F32),
+            pltpu.VMEM((256, 256), F32),
+            pltpu.VMEM((4, 256, 256), F32),
+            pltpu.VMEM((E, BLOCK * BLOCK), BF16),
+            pltpu.VMEM((E, BLOCK * BLOCK), BF16),
+            pltpu.VMEM((E, BLOCK * BLOCK), BF16),
+            pltpu.VMEM((vectors, E, BLOCK), F32),
+            pltpu.VMEM((vectors, E, BLOCK), F32),
+            pltpu.VMEM((E * 8, 128), F32),
+            pltpu.VMEM((E * 8, 128), F32),
+            pltpu.VMEM((E * BLOCK, 128), F32),
+            pltpu.VMEM((E * BLOCK, 128), F32),
+            pltpu.VMEM((E, BLOCK, 128), BF16),
+            pltpu.VMEM((E, BLOCK, 128), BF16),
             pltpu.VMEM((3, EX, EY, 8, 128), F32),
             pltpu.VMEM((3, 2, EY, 8, 128), F32),
             pltpu.VMEM((3, 2, EX, 8, 128), F32),
@@ -332,23 +454,35 @@
             pltpu.VMEM((E * BLOCK, 256), BF16),
             pltpu.VMEM((4, 512, 256), BF16),
             pltpu.VMEM((E, 8, 128), F32),
+            pltpu.SemaphoreType.DMA((5,)),
+            pltpu.SemaphoreType.DMA((6,)),
             pltpu.SemaphoreType.DMA((4, 4)),
             pltpu.SemaphoreType.DMA((4, 4)),
         ],
         compiler_params=pltpu.CompilerParams(
-            collective_id=0, has_side_effects=True, vmem_limit_bytes=32 * 1024 * 1024
+            collective_id=0, has_side_effects=True, vmem_limit_bytes=VMEM_LIMIT
         ),
         name="galerkin_smooth",
     )(
         bounds,
         aggregate.reshape(E),
         ghost_labels.reshape(2 * EY + 2 * EX),
-        matrix,
-        twice,
-        by_element(rhs),
-        by_element(guess),
-    )
-    smoothed = smoothed[:, :vectors, :BLOCK].transpose(1, 2, 0)
+        blocks.reshape(E, BLOCK * BLOCK),
+        faces.reshape(E, BLOCK * BLOCK),
+        tentative.reshape(E, BLOCK * BLOCK),
+        values_last(rhs),
+        values_last(guess),
+    )
+    smoothed, local, ghost = pl.pallas_call(
+        store_kernel,
+        out_shape=shapes,
+        in_specs=[hbm] * 3,
+        out_specs=(hbm, hbm, hbm),
+        scratch_shapes=[pltpu.SemaphoreType.DMA((6,))],
+        compiler_params=pltpu.CompilerParams(vmem_limit_bytes=VMEM_LIMIT),
+        name="store_results",
+    )(smoothed, local, ghost)
+    smoothed = smoothed.transpose(0, 2, 1)
     return (smoothed[None, None], local[None, None], ghost[None, None])
 
 

time: 28.2 us -> 62.5 us (2.22)
  Pallas kernels: 17.1 us -> 61.7 us
  local copies, waits for them, and re-layouts: 9.51 us -> 0 us
    pallas_call x1 -> x2, Pallas kernels: 17.1 us -> 61.7 us  [the longest x1 43.8 us: on_device(): pl.pallas_call(store_kernel, out_shape=shapes, in_specs=[hbm] * 3, out_sp...]
    unnamed x20 -> x0, local copies, waits for them, and re-layouts: 6.78 us -> none
    transpose x1 -> x0, local copies, waits for them, and re-layouts: 1.35 us -> none  [on_device(): faces.reshape(E, 4, BLOCK, 16).transpose(0, 2, 1, 3)]
    reshape x3 -> x0, local copies, waits for them, and re-layouts: 1.34 us -> none  [the longest x1 0.54 us: on_device(): diag = blocks.reshape(E, BLOCK, BLOCK)]
where the time goes in v2:
time: 62.5 us; the launch traced here: 62.4 us
  Pallas kernels  61.7 us (99%)
  between operations  0.64 us (1%)
    pallas_call x1, Pallas kernels, on_device(): pl.pallas_call(store_kernel, out_shape=shapes, in_specs=[hbm] * 3, out_sp...  43.8 us
    pallas_call x1, Pallas kernels, on_device(): pl.pallas_call(lambda *refs: kernel(nx, ny, *refs), out_shape=shapes, in_...  17.9 us

profile of v2, /device:TPU:0, one launch (start us, length us, event | category | flops | bytes accessed | tf_op | source)
XLA Modules:
  0.0 62.4 jit_solution(4604907691829624651)
XLA Ops:
  0.6 17.9 %galerkin_smooth.1 = (f32[6,32,64]{2,1,0:T(8,128)}, f32[256,256]{1,0:T(8,128)}, f32[4,256,256]{2,1,0:T(8,128)}) custom-call(f32[2]{0:T(128)} %refs_0_.1, s32[32]{0:T(128)} %bitcast.21, s32[24]{0:T(128)} %bitcast.22, bf16[32,4096]{1,0:T(8,128)(2,1)} %bitcast.16, bf16[32,4096]{1,0:T(8,128)(2,1)} %bitcast.17, bf16[32,4096]{1,0:T(8,128)(2,1)} %bitcast.18, ...), custom_call_target="tpu_custom_call" | custom-call | tf_op jit(solution)/shard_map/galerkin_smooth/pallas_call | solution.py:426
  18.5 43.8 %store_results.1 = (f32[6,32,64]{2,1,0:T(8,128)}, f32[256,256]{1,0:T(8,128)}, f32[4,256,256]{2,1,0:T(8,128)}) custom-call(f32[6,32,64]{2,1,0:T(8,128)} %get-tuple-element.9.smoothed, f32[256,256]{1,0:T(8,128)} %get-tuple-element.10.local, f32[4,256,256]{2,1,0:T(8,128)} %get-tuple-element.11.ghost), custom_call_target="tpu_custom_call" | custom-call | tf_op jit(solution)/shard_map/store_results/pallas_call | solution.py:476

commit v3 on v2

--- a/solution.py
+++ b/solution.py
@@ -56,7 +56,8 @@
     gbuf,
     hx,
     hy,
-    tg,
+    ty32,
+    ty,
     thx,
     thy,
     tat,
@@ -120,11 +121,13 @@
         )
 
     def tent_copy(f):
-        rows = pl.ds(16 * f, 16)
-        if f < 2:
-            src, dst = tg.at[EX - 1 if f == 0 else 0, :, rows], thx.at[f]
+        if f == 0:
+            src = t_ref.at[E - EY : E, BLOCK - 16 : BLOCK]
+        elif f == 1:
+            src = t_ref.at[0:EY, 0:16]
         else:
-            src, dst = tg.at[:, EY - 1 if f == 2 else 0, rows], thy.at[f - 2]
+            src = ty.at[f - 2, :, EY - 1 if f == 2 else 0]
+        dst = thx.at[f] if f < 2 else thy.at[f - 2]
         return pltpu.make_async_remote_copy(
             src_ref=src,
             dst_ref=dst,
@@ -161,6 +164,8 @@
         (col >= BLOCK) & (row == trace_source(col - BLOCK)), 1.0, 0.0
     ).astype(BF16)
     lane = lax.broadcasted_iota(jnp.int32, (1, 1, 1, 128), 3)
+
+    left8 = lax.broadcasted_iota(jnp.int32, (8, 128), 1) < BLOCK
 
     def split(values):
         high = values.astype(BF16)
@@ -189,14 +194,20 @@
         )
         full = field + near.reshape(E, 8, 128)
         high, low = split(full)
-        for e in range(E):
+        for g in range(E // 4):
+            group = range(4 * g, 4 * g + 4)
             both = lax.dot_general(
-                jnp.concatenate([high[e], low[e]], axis=0),
-                m_ref[e],
+                jnp.concatenate([half[e] for e in group for half in (high, low)], axis=0),
+                m_ref[4 * g : 4 * g + 4].reshape(4 * BLOCK, 128),
                 NT,
                 preferred_element_type=F32,
             )
-            obuf[e, :, :BLOCK] = both[:8] + both[8:]
+            for k, e in enumerate(group):
+                tile = both[16 * k : 16 * (k + 1), 128 * (k // 2) : 128 * (k // 2 + 1)]
+                part = tile[:8] + tile[8:]
+                if k % 2:
+                    part = pltpu.roll(part, BLOCK, 1)
+                obuf[e] = jnp.where(left8, part, 0.0)
         return obuf[...]
 
     vectors = guess_in.shape[0]
@@ -209,7 +220,6 @@
             )
         return target[...].reshape(E, 8, 128)
 
-    obuf[...] = jnp.zeros_like(obuf)
     for f in range(4):
 
         @pl.when(jnp.logical_not(has_from[f]))
@@ -238,11 +248,12 @@
         trows32[pl.ds(2 * c + 1, E, stride=BLOCK), :] = jnp.where(left, odd, even)
     t_ref[...] = trows32[...].reshape(E, BLOCK, 128).astype(BF16)
 
-    row = lax.broadcasted_iota(jnp.int32, (BLOCK, BLOCK), 0)
-    col = lax.broadcasted_iota(jnp.int32, (BLOCK, BLOCK), 1)
-    pick = jnp.where(col == trace_source(row), 1.0, 0.0).astype(BF16)
-    for e in range(E):
-        tg[e // EY, e % EY] = jnp.dot(pick, t_ref[e], preferred_element_type=F32).astype(BF16)
+    for s in range(2):
+        for k in range(4):
+            ty32[s, pl.ds(k, 4 * E, stride=4), :] = trows32[
+                pl.ds((12 if s == 0 else 0) + k, 4 * E, stride=16), :
+            ]
+    ty[...] = ty32[...].reshape(2, EX, EY, 16, 128).astype(BF16)
     start(tent_copy)
 
     row = lax.broadcasted_iota(jnp.int32, (512, 512), 0)
@@ -305,7 +316,12 @@
         near = [zero16] * 4
         for f, (jx, jy) in enumerate(((ix - 1, iy), (ix + 1, iy), (ix, iy - 1), (ix, iy + 1))):
             if 0 <= jx < EX and 0 <= jy < EY:
-                near[f] = wide(tg[jx, jy, 16 * f : 16 * f + 16]) * mask(labels[jx * EY + jy])
+                j = jx * EY + jy
+                if f < 2:
+                    rows = t_ref[j, BLOCK - 16 : BLOCK] if f == 0 else t_ref[j, 0:16]
+                else:
+                    rows = ty[f - 2, jx, jy]
+                near[f] = wide(rows) * mask(labels[j])
         stacked = jnp.concatenate([own] + near, axis=0)
         x = jnp.dot(m_ref[e], stacked, preferred_element_type=F32)
         high, low = split(x)
@@ -398,16 +414,20 @@
     wait_send(tent_copy)
 
 
-def store_kernel(smoothed, local, ghost, smoothed_out, local_out, ghost_out, sem):
-    pairs = [(ghost.at[f], ghost_out.at[f]) for f in range(4)]
-    pairs += [(local, local_out), (smoothed, smoothed_out)]
-    copies = [
-        pltpu.make_async_copy(src, dst, sem.at[i]) for i, (src, dst) in enumerate(pairs)
-    ]
-    for copy in copies:
-        copy.start()
-    for copy in copies:
-        copy.wait()
+def store_kernel(
+    smoothed, local, ghost, smoothed_out, local_out, ghost_out, field, square, wide, in_sem, out_sem
+):
+    pieces = [(ghost.at[f], wide.at[f], ghost_out.at[f]) for f in range(4)]
+    pieces += [(local, square, local_out), (smoothed, field, smoothed_out)]
+    loads = [pltpu.make_async_copy(p[0], p[1], in_sem.at[i]) for i, p in enumerate(pieces)]
+    stores = [pltpu.make_async_copy(p[1], p[2], out_sem.at[i]) for i, p in enumerate(pieces)]
+    for load in loads:
+        load.start()
+    for load, store in zip(loads, stores):
+        load.wait()
+        store.start()
+    for store in stores:
+        store.wait()
 
 
 def on_device(nx, ny, blocks, faces, tentative, aggregate, ghost_labels, rhs, guess, bounds):
@@ -446,7 +466,8 @@
             pltpu.VMEM((3, EX, EY, 8, 128), F32),
             pltpu.VMEM((3, 2, EY, 8, 128), F32),
             pltpu.VMEM((3, 2, EX, 8, 128), F32),
-            pltpu.VMEM((EX, EY, BLOCK, 128), BF16),
+            pltpu.VMEM((2, 16 * E, 128), F32),
+            pltpu.VMEM((2, EX, EY, 16, 128), BF16),
             pltpu.VMEM((2, EY, 16, 128), BF16),
             pltpu.VMEM((2, EX, 16, 128), BF16),
             pltpu.VMEM((256, E * BLOCK), BF16),
@@ -478,7 +499,13 @@
         out_shape=shapes,
         in_specs=[hbm] * 3,
         out_specs=(hbm, hbm, hbm),
-        scratch_shapes=[pltpu.SemaphoreType.DMA((6,))],
+        scratch_shapes=[
+            pltpu.VMEM((vectors, E, BLOCK), F32),
+            pltpu.VMEM((256, 256), F32),
+            pltpu.VMEM((4, 256, 256), F32),
+            pltpu.SemaphoreType.DMA((6,)),
+            pltpu.SemaphoreType.DMA((6,)),
+        ],
         compiler_params=pltpu.CompilerParams(vmem_limit_bytes=VMEM_LIMIT),
         name="store_results",
     )(smoothed, local, ghost)

time: 62.5 us -> 20.7 us (0.33)
  Pallas kernels: 61.7 us -> 19.9 us
    pallas_call x1, Pallas kernels: 43.8 us -> 2.13 us  [on_device(): pl.pallas_call(store_kernel, out_shape=shapes, in_specs=[hbm] * 3, out_sp...]
where the time goes in v3:
time: 20.7 us; the launch traced here: 20.6 us
  Pallas kernels  19.9 us (96%)
  between operations  0.64 us (3%)
    pallas_call x1, Pallas kernels, on_device(): pl.pallas_call(lambda *refs: kernel(nx, ny, *refs), out_shape=shapes, in_...  17.8 us
    pallas_call x1, Pallas kernels, on_device(): pl.pallas_call(store_kernel, out_shape=shapes, in_specs=[hbm] * 3, out_sp...  2.13 us

profile of v3, /device:TPU:0, one launch (start us, length us, event | category | flops | bytes accessed | tf_op | source)
XLA Modules:
  0.0 20.6 jit_solution(13585657205938304068)
XLA Ops:
  0.6 17.8 %galerkin_smooth.1 = (f32[6,32,64]{2,1,0:T(8,128)}, f32[256,256]{1,0:T(8,128)}, f32[4,256,256]{2,1,0:T(8,128)}) custom-call(f32[2]{0:T(128)} %refs_0_.1, s32[32]{0:T(128)} %bitcast.21, s32[24]{0:T(128)} %bitcast.22, bf16[32,4096]{1,0:T(8,128)(2,1)} %bitcast.16, bf16[32,4096]{1,0:T(8,128)(2,1)} %bitcast.17, bf16[32,4096]{1,0:T(8,128)(2,1)} %bitcast.18, ...), custom_call_target="tpu_custom_call" | custom-call | tf_op jit(solution)/shard_map/galerkin_smooth/pallas_call | solution.py:446
  18.4 2.1 %store_results.1 = (f32[6,32,64]{2,1,0:T(8,128)}, f32[256,256]{1,0:T(8,128)}, f32[4,256,256]{2,1,0:T(8,128)}) custom-call(f32[6,32,64]{2,1,0:T(8,128)} %get-tuple-element.9.smoothed, f32[256,256]{1,0:T(8,128)} %get-tuple-element.10.local, f32[4,256,256]{2,1,0:T(8,128)} %get-tuple-element.11.ghost), custom_call_target="tpu_custom_call" | custom-call | tf_op jit(solution)/shard_map/store_results/pallas_call | solution.py:497

commit v4 on v3

--- a/solution.py
+++ b/solution.py
@@ -28,9 +28,9 @@
 def kernel(
     nx,
     ny,
-    bounds,
-    labels,
-    ghost_labels,
+    bounds_hbm,
+    labels_hbm,
+    ghost_labels_hbm,
     blocks_hbm,
     faces_hbm,
     tent_hbm,
@@ -42,6 +42,9 @@
     out_ref,
     local_ref,
     ghost_ref,
+    bounds,
+    labels,
+    ghost_labels,
     blocks_in,
     faces_in,
     tent_in,
@@ -54,15 +57,14 @@
     m_ref,
     t_ref,
     gbuf,
-    hx,
-    hy,
+    packed,
+    halo,
     ty32,
     ty,
     thx,
     thy,
     tat,
-    xh,
-    xl,
+    xb,
     xg,
     obuf,
     load_sem,
@@ -79,6 +81,9 @@
                 (faces_hbm, faces_in),
                 (blocks_hbm, blocks_in),
                 (rhs_hbm, rhs_in),
+                (bounds_hbm, bounds),
+                (labels_hbm, labels),
+                (ghost_labels_hbm, ghost_labels),
             )
         )
     ]
@@ -107,13 +112,9 @@
             )
 
     def field_copy(r, f):
-        if f < 2:
-            src, dst = gbuf.at[r, EX - 1 if f == 0 else 0], hx.at[r, f]
-        else:
-            src, dst = gbuf.at[r, :, EY - 1 if f == 2 else 0], hy.at[r, f - 2]
         return pltpu.make_async_remote_copy(
-            src_ref=src,
-            dst_ref=dst,
+            src_ref=packed.at[r, f],
+            dst_ref=halo.at[r, f],
             send_sem=send_sem.at[r, f],
             recv_sem=recv_sem.at[r, f],
             device_id=target[f],
@@ -167,6 +168,23 @@
 
     left8 = lax.broadcasted_iota(jnp.int32, (8, 128), 1) < BLOCK
 
+    slot = lax.broadcasted_iota(jnp.int32, (8, 128), 1) >> 4
+    edge = (
+        [(EX - 1, iy) for iy in range(EY)],
+        [(0, iy) for iy in range(EY)],
+        [(ix, EY - 1) for ix in range(EX)],
+        [(ix, 0) for ix in range(EX)],
+    )
+
+    def unpack(r, f):
+        tile = halo[r, f]
+        return jnp.stack(
+            [
+                pltpu.roll(tile, (BLOCK + 16 * f - 16 * i) % 128, 1)
+                for i in range(len(edge[f]))
+            ]
+        )
+
     def split(values):
         high = values.astype(BF16)
         low = (values - high.astype(F32)).astype(BF16)
@@ -177,7 +195,14 @@
         both = jnp.dot(
             jnp.concatenate([high, low], axis=0), gather, preferred_element_type=F32
         )
-        gbuf[r] = (both[: E * 8] + both[E * 8 :]).reshape(EX, EY, 8, 128)
+        traces = (both[: E * 8] + both[E * 8 :]).reshape(EX, EY, 8, 128)
+        gbuf[r] = traces
+        for f in range(4):
+            tile = jnp.zeros((8, 128), F32)
+            for i, (ix, iy) in enumerate(edge[f]):
+                moved = pltpu.roll(traces[ix, iy], (16 * i + BLOCK - 16 * f) % 128, 1)
+                tile = jnp.where(slot == i, moved, tile)
+            packed[r, f] = tile
         if r == 0:
             pl.semaphore_wait(barrier, count)
         start(lambda f: field_copy(r, f))
@@ -185,13 +210,14 @@
     def operate(r, field):
         wait_recv(lambda f: field_copy(r, f))
         own = gbuf[r]
-        from0 = jnp.concatenate([hx[r, 0][None], own[:-1]], axis=0)
-        from1 = jnp.concatenate([own[1:], hx[r, 1][None]], axis=0)
-        from2 = jnp.concatenate([hy[r, 0][:, None], own[:, :-1]], axis=1)
-        from3 = jnp.concatenate([own[:, 1:], hy[r, 1][:, None]], axis=1)
+        from0 = jnp.concatenate([unpack(r, 0)[None], own[:-1]], axis=0)
+        from1 = jnp.concatenate([own[1:], unpack(r, 1)[None]], axis=0)
+        from2 = jnp.concatenate([unpack(r, 2)[:, None], own[:, :-1]], axis=1)
+        from3 = jnp.concatenate([own[:, 1:], unpack(r, 3)[:, None]], axis=1)
         near = jnp.where(
             lane < 80, from0, jnp.where(lane < 96, from1, jnp.where(lane < 112, from2, from3))
         )
+        near = jnp.where(lane < BLOCK, 0.0, near)
         full = field + near.reshape(E, 8, 128)
         high, low = split(full)
         for g in range(E // 4):
@@ -224,11 +250,10 @@
 
         @pl.when(jnp.logical_not(has_from[f]))
         def _(f=f):
+            halo[:, f] = jnp.zeros((3, 8, 128), F32)
             if f < 2:
-                hx[:, f] = jnp.zeros((3, EY, 8, 128), F32)
                 thx[f] = jnp.zeros((EY, 16, 128), BF16)
             else:
-                hy[:, f - 2] = jnp.zeros((3, EX, 8, 128), F32)
                 thy[f - 2] = jnp.zeros((EX, 16, 128), BF16)
 
     loads[0].wait()
@@ -280,6 +305,8 @@
         rows32[pl.ds(2 * c + 1, E, stride=BLOCK), :] = jnp.where(left, turn(own), side)
     m_ref[...] = rows32[...].reshape(E, BLOCK, 128).astype(BF16)
 
+    for load in loads[5:]:
+        load.wait()
     low_b = jnp.full((1, 1, 128), bounds[0], F32)
     high_b = jnp.full((1, 1, 128), bounds[1], F32)
     centre = 0.5 * (high_b + low_b)
@@ -324,9 +351,7 @@
                 near[f] = wide(rows) * mask(labels[j])
         stacked = jnp.concatenate([own] + near, axis=0)
         x = jnp.dot(m_ref[e], stacked, preferred_element_type=F32)
-        high, low = split(x)
-        xh[BLOCK * e : BLOCK * (e + 1)] = high
-        xl[BLOCK * e : BLOCK * (e + 1)] = low
+        xb[BLOCK * e : BLOCK * (e + 1)] = x.astype(BF16)
 
     loads[4].wait()
     rhs = by_element(rhs_in, rhs_ref)
@@ -359,9 +384,7 @@
     send_traces(2, update)
     answer = answer + update
 
-    local_ref[...] = jnp.dot(tat[...], xh[...], preferred_element_type=F32) + jnp.dot(
-        tat[...], xl[...], preferred_element_type=F32
-    )
+    local_ref[...] = jnp.dot(tat[...], xb[...], preferred_element_type=F32)
 
     stores[4].start()
 
@@ -436,7 +459,6 @@
     def values_last(field):
         return field.reshape(vectors, BLOCK, E).transpose(0, 2, 1)
 
-    smem = pl.BlockSpec(memory_space=pltpu.SMEM)
     hbm = pl.BlockSpec(memory_space=pltpu.HBM)
     shapes = (
         jax.ShapeDtypeStruct((vectors, E, BLOCK), F32),
@@ -446,12 +468,15 @@
     smoothed, local, ghost = pl.pallas_call(
         lambda *refs: kernel(nx, ny, *refs),
         out_shape=shapes,
-        in_specs=[smem] * 3 + [hbm] * 5,
+        in_specs=[hbm] * 8,
         out_specs=(hbm, hbm, hbm),
         scratch_shapes=[
             pltpu.VMEM((vectors, E, BLOCK), F32),
             pltpu.VMEM((256, 256), F32),
             pltpu.VMEM((4, 256, 256), F32),
+            pltpu.SMEM((2,), F32),
+            pltpu.SMEM((E,), jnp.int32),
+            pltpu.SMEM((2 * EY + 2 * EX,), jnp.int32),
             pltpu.VMEM((E, BLOCK * BLOCK), BF16),
             pltpu.VMEM((E, BLOCK * BLOCK), BF16),
             pltpu.VMEM((E, BLOCK * BLOCK), BF16),
@@ -464,18 +489,17 @@
             pltpu.VMEM((E, BLOCK, 128), BF16),
             pltpu.VMEM((E, BLOCK, 128), BF16),
             pltpu.VMEM((3, EX, EY, 8, 128), F32),
-            pltpu.VMEM((3, 2, EY, 8, 128), F32),
-            pltpu.VMEM((3, 2, EX, 8, 128), F32),
+            pltpu.VMEM((3, 4, 8, 128), F32),
+            pltpu.VMEM((3, 4, 8, 128), F32),
             pltpu.VMEM((2, 16 * E, 128), F32),
             pltpu.VMEM((2, EX, EY, 16, 128), BF16),
             pltpu.VMEM((2, EY, 16, 128), BF16),
             pltpu.VMEM((2, EX, 16, 128), BF16),
             pltpu.VMEM((256, E * BLOCK), BF16),
             pltpu.VMEM((E * BLOCK, 256), BF16),
-            pltpu.VMEM((E * BLOCK, 256), BF16),
             pltpu.VMEM((4, 512, 256), BF16),
             pltpu.VMEM((E, 8, 128), F32),
-            pltpu.SemaphoreType.DMA((5,)),
+            pltpu.SemaphoreType.DMA((8,)),
             pltpu.SemaphoreType.DMA((6,)),
             pltpu.SemaphoreType.DMA((4, 4)),
             pltpu.SemaphoreType.DMA((4, 4)),

time: 20.7 us -> 18.1 us (0.87)
  Pallas kernels: 19.9 us -> 17.2 us
    pallas_call x1, Pallas kernels: 17.8 us -> 15.1 us  [on_device(): pl.pallas_call(lambda *refs: kernel(nx, ny, *refs), out_shape=shapes, in_...]
where the time goes in v4:
time: 18.1 us; the launch traced here: 17.9 us
  Pallas kernels  17.2 us (95%)
  between operations  0.64 us (4%)
    pallas_call x1, Pallas kernels, on_device(): pl.pallas_call(lambda *refs: kernel(nx, ny, *refs), out_shape=shapes, in_...  15.1 us
    pallas_call x1, Pallas kernels, on_device(): pl.pallas_call(store_kernel, out_shape=shapes, in_specs=[hbm] * 3, out_sp...  2.13 us

profile of v4, /device:TPU:0, one launch (start us, length us, event | category | flops | bytes accessed | tf_op | source)
XLA Modules:
  0.0 17.9 jit_solution(3631739310787820756)
XLA Ops:
  0.6 15.1 %galerkin_smooth.1 = (f32[6,32,64]{2,1,0:T(8,128)}, f32[256,256]{1,0:T(8,128)}, f32[4,256,256]{2,1,0:T(8,128)}) custom-call(f32[2]{0:T(128)} %refs_0_.1, s32[32]{0:T(128)} %bitcast.21, s32[24]{0:T(128)} %bitcast.22, bf16[32,4096]{1,0:T(8,128)(2,1)} %bitcast.16, bf16[32,4096]{1,0:T(8,128)(2,1)} %bitcast.17, bf16[32,4096]{1,0:T(8,128)(2,1)} %bitcast.18, ...), custom_call_target="tpu_custom_call" | custom-call | tf_op jit(solution)/shard_map/galerkin_smooth/pallas_call | solution.py:468
  15.8 2.1 %store_results.1 = (f32[6,32,64]{2,1,0:T(8,128)}, f32[256,256]{1,0:T(8,128)}, f32[4,256,256]{2,1,0:T(8,128)}) custom-call(f32[6,32,64]{2,1,0:T(8,128)} %get-tuple-element.9.smoothed, f32[256,256]{1,0:T(8,128)} %get-tuple-element.10.local, f32[4,256,256]{2,1,0:T(8,128)} %get-tuple-element.11.ghost), custom_call_target="tpu_custom_call" | custom-call | tf_op jit(solution)/shard_map/store_results/pallas_call | solution.py:521

commit v5 on v4

--- a/solution.py
+++ b/solution.py
@@ -67,6 +67,8 @@
     xb,
     xg,
     obuf,
+    order,
+    masks,
     load_sem,
     store_sem,
     send_sem,
@@ -239,7 +241,6 @@
     vectors = guess_in.shape[0]
 
     def by_element(source, target):
-        target[...] = jnp.zeros_like(target)
         for n in range(vectors):
             target[pl.ds(n, E, stride=8), :] = jnp.concatenate(
                 [source[n], jnp.zeros((E, BLOCK), F32)], axis=1
@@ -256,6 +257,15 @@
             else:
                 thy[f - 2] = jnp.zeros((EX, 16, 128), BF16)
 
+    row = lax.broadcasted_iota(jnp.int32, (512, 512), 0)
+    col = lax.broadcasted_iota(jnp.int32, (512, 512), 1)
+    source = (((col >> 4) & 3) << 7) + ((col >> 6) << 4) + (col & 15)
+    order[...] = jnp.where(row == source, 1.0, 0.0).astype(BF16)
+    group = lax.broadcasted_iota(jnp.int32, (16, 256), 1) >> 6
+    for b in range(NAGG):
+        masks[b] = jnp.where(group == b, 1.0, 0.0).astype(BF16)
+    guess_ref[...] = jnp.zeros_like(guess_ref)
+    rhs_ref[...] = jnp.zeros_like(rhs_ref)
     loads[0].wait()
     guess = by_element(guess_in, guess_ref)
     send_traces(0, guess)
@@ -281,10 +291,6 @@
     ty[...] = ty32[...].reshape(2, EX, EY, 16, 128).astype(BF16)
     start(tent_copy)
 
-    row = lax.broadcasted_iota(jnp.int32, (512, 512), 0)
-    col = lax.broadcasted_iota(jnp.int32, (512, 512), 1)
-    source = (((col >> 4) & 3) << 7) + ((col >> 6) << 4) + (col & 15)
-    order = jnp.where(row == source, 1.0, 0.0).astype(BF16)
     loads[2].wait()
     grouped = jnp.concatenate(
         [
@@ -296,7 +302,7 @@
         ],
         axis=0,
     )
-    couple = jnp.dot(grouped, order, preferred_element_type=F32)
+    couple = jnp.dot(grouped, order[...], preferred_element_type=F32)
     loads[3].wait()
     for c in range(E):
         own = blocks_in[:, 128 * c : 128 * (c + 1)].astype(F32)
@@ -327,11 +333,6 @@
     lane3 = lax.broadcasted_iota(jnp.int32, (1, 1, 128), 2)
     inverse = jnp.where(lane3 < BLOCK, 1.0 / jnp.where(lane3 < BLOCK, diagonal, 1.0), 0.0)
 
-    group = lax.broadcasted_iota(jnp.int32, (1, 256), 1) >> 6
-
-    def mask(label):
-        return jnp.where(group == label, 1.0, 0.0).astype(BF16)
-
     def wide(half):
         return jnp.concatenate([half, half], axis=1)
 
@@ -339,7 +340,8 @@
 
     def products(e):
         ix, iy = e // EY, e % EY
-        own = wide(t_ref[e]) * mask(labels[e])
+        own = wide(t_ref[e]).reshape(4, 16, 256) * masks[labels[e]][None]
+        own = own.reshape(BLOCK, 256)
         near = [zero16] * 4
         for f, (jx, jy) in enumerate(((ix - 1, iy), (ix + 1, iy), (ix, iy - 1), (ix, iy + 1))):
             if 0 <= jx < EX and 0 <= jy < EY:
@@ -348,7 +350,7 @@
                     rows = t_ref[j, BLOCK - 16 : BLOCK] if f == 0 else t_ref[j, 0:16]
                 else:
                     rows = ty[f - 2, jx, jy]
-                near[f] = wide(rows) * mask(labels[j])
+                near[f] = wide(rows) * masks[labels[j]]
         stacked = jnp.concatenate([own] + near, axis=0)
         x = jnp.dot(m_ref[e], stacked, preferred_element_type=F32)
         xb[BLOCK * e : BLOCK * (e + 1)] = x.astype(BF16)
@@ -391,34 +393,59 @@
     wait_recv(tent_copy)
     zero64 = jnp.zeros((BLOCK, 256), BF16)
 
-    def ghost_product(f, e, rows, label):
-        near = [zero16] * 4
-        near[f] = wide(rows) * mask(label)
-        stacked = jnp.concatenate([zero64] + near, axis=0)
-        return jnp.dot(m_ref[e], stacked, preferred_element_type=F32).astype(BF16)
+    left_b = jnp.where(lax.broadcasted_iota(jnp.int32, (16, 128), 1) < BLOCK, 1.0, 0.0)
+    right_b = (1.0 - left_b).astype(BF16)
+    left_b = left_b.astype(BF16)
+    left64 = lax.broadcasted_iota(jnp.int32, (BLOCK, 128), 1) < BLOCK
+
+    def ghost_products(f, elements, rows, numbers):
+        near = jnp.concatenate(
+            [rows[2 * h] * left_b + rows[2 * h + 1] * right_b for h in range(2)], axis=1
+        )
+        faces_near = [zero16] * 4
+        faces_near[f] = near
+        stacked = jnp.concatenate([zero64] + faces_near, axis=0)
+        matrix = jnp.concatenate([m_ref[e] for e in elements], axis=0)
+        both = jnp.dot(matrix, stacked, preferred_element_type=F32)
+        results = []
+        for k in range(4):
+            x = both[BLOCK * k : BLOCK * (k + 1), 128 * (k // 2) : 128 * (k // 2 + 1)]
+            other = turn(x)
+            x = jnp.where(left64, x, other) if k % 2 == 0 else jnp.where(left64, other, x)
+            x = wide(x.astype(BF16)).reshape(4, 16, 256) * masks[ghost_labels[numbers[k]]][None]
+            results.append(x.reshape(BLOCK, 256))
+        return results
 
     for f in range(2):
-        for iy in range(EY):
-            e = (0 if f == 0 else EX - 1) * EY + iy
-            xg[f, BLOCK * iy : BLOCK * (iy + 1)] = ghost_product(
-                f, e, thx[f, iy], ghost_labels[f * EY + iy]
-            )
-        first = 0 if f == 0 else (EX - 1) * EY * BLOCK
+        first = 0 if f == 0 else (EX - 1) * EY
+        for h in range(0, EY, 4):
+            parts = ghost_products(
+                f,
+                [first + h + k for k in range(4)],
+                [thx[f, h + k] for k in range(4)],
+                [f * EY + h + k for k in range(4)],
+            )
+            for k in range(4):
+                xg[f, BLOCK * (h + k) : BLOCK * (h + k + 1)] = parts[k]
         ghost_ref[f] = jnp.dot(
-            tat[:, first : first + EY * BLOCK], xg[f], preferred_element_type=F32
+            tat[:, first * BLOCK : (first + EY) * BLOCK], xg[f], preferred_element_type=F32
         )
         stores[f].start()
     for f in range(2, 4):
+        column = 0 if f == 2 else EY - 1
+        parts = ghost_products(
+            f,
+            [ix * EY + column for ix in range(EX)],
+            [thy[f - 2, ix] for ix in range(EX)],
+            [2 * EY + (f - 2) * EX + ix for ix in range(EX)],
+        )
         total = None
         for ix in range(EX):
-            e = ix * EY + (0 if f == 2 else EY - 1)
-            x = ghost_product(f, e, thy[f - 2, ix], ghost_labels[2 * EY + (f - 2) * EX + ix])
-            parts = [x, zero64] if f == 2 else [zero64, x]
-            xg[f, 128 * ix : 128 * (ix + 1)] = jnp.concatenate(parts, axis=0)
-            first = 128 * (e // 2)
+            pair = [parts[ix], zero64] if f == 2 else [zero64, parts[ix]]
+            first = 128 * ((ix * EY + column) // 2)
             part = jnp.dot(
                 tat[:, first : first + 128],
-                xg[f, 128 * ix : 128 * (ix + 1)],
+                jnp.concatenate(pair, axis=0),
                 preferred_element_type=F32,
             )
             total = part if total is None else total + part
@@ -499,6 +526,8 @@
             pltpu.VMEM((E * BLOCK, 256), BF16),
             pltpu.VMEM((4, 512, 256), BF16),
             pltpu.VMEM((E, 8, 128), F32),
+            pltpu.VMEM((512, 512), BF16),
+            pltpu.VMEM((NAGG, 16, 256), BF16),
             pltpu.SemaphoreType.DMA((8,)),
             pltpu.SemaphoreType.DMA((6,)),
             pltpu.SemaphoreType.DMA((4, 4)),

time: 18.1 us -> 18.1 us (level)
  no operation moved by 1% of the time
where the time goes in v5:
time: 18.1 us; the launch traced here: 17.9 us
  Pallas kernels  17.2 us (95%)
  between operations  0.64 us (4%)
    pallas_call x1, Pallas kernels, on_device(): pl.pallas_call(lambda *refs: kernel(nx, ny, *refs), out_shape=shapes, in_...  15.1 us
    pallas_call x1, Pallas kernels, on_device(): pl.pallas_call(store_kernel, out_shape=shapes, in_specs=[hbm] * 3, out_sp...  2.13 us

profile of v5, /device:TPU:0, one launch (start us, length us, event | category | flops | bytes accessed | tf_op | source)
XLA Modules:
  0.0 17.9 jit_solution(2799271955997907185)
XLA Ops:
  0.6 15.1 %galerkin_smooth.1 = (f32[6,32,64]{2,1,0:T(8,128)}, f32[256,256]{1,0:T(8,128)}, f32[4,256,256]{2,1,0:T(8,128)}) custom-call(f32[2]{0:T(128)} %refs_0_.1, s32[32]{0:T(128)} %bitcast.21, s32[24]{0:T(128)} %bitcast.22, bf16[32,4096]{1,0:T(8,128)(2,1)} %bitcast.16, bf16[32,4096]{1,0:T(8,128)(2,1)} %bitcast.17, bf16[32,4096]{1,0:T(8,128)(2,1)} %bitcast.18, ...), custom_call_target="tpu_custom_call" | custom-call | tf_op jit(solution)/shard_map/galerkin_smooth/pallas_call | solution.py:495
  15.8 2.1 %store_results.1 = (f32[6,32,64]{2,1,0:T(8,128)}, f32[256,256]{1,0:T(8,128)}, f32[4,256,256]{2,1,0:T(8,128)}) custom-call(f32[6,32,64]{2,1,0:T(8,128)} %get-tuple-element.9.smoothed, f32[256,256]{1,0:T(8,128)} %get-tuple-element.10.local, f32[4,256,256]{2,1,0:T(8,128)} %get-tuple-element.11.ghost), custom_call_target="tpu_custom_call" | custom-call | tf_op jit(solution)/shard_map/store_results/pallas_call | solution.py:550

commit v6 on v5

--- a/solution.py
+++ b/solution.py
@@ -79,10 +79,10 @@
         for i, (src, dst) in enumerate(
             (
                 (guess_hbm, guess_in),
-                (tent_hbm, tent_in),
                 (faces_hbm, faces_in),
                 (blocks_hbm, blocks_in),
                 (rhs_hbm, rhs_in),
+                (tent_hbm, tent_in),
                 (bounds_hbm, bounds),
                 (labels_hbm, labels),
                 (ghost_labels_hbm, ghost_labels),
@@ -275,23 +275,8 @@
     def turn(values):
         return pltpu.roll(values, BLOCK, 1)
 
+
     loads[1].wait()
-    for c in range(E):
-        even = tent_in[:, 128 * c : 128 * (c + 1)].astype(F32)
-        odd = turn(even)
-        trows32[pl.ds(2 * c, E, stride=BLOCK), :] = jnp.where(left, even, odd)
-        trows32[pl.ds(2 * c + 1, E, stride=BLOCK), :] = jnp.where(left, odd, even)
-    t_ref[...] = trows32[...].reshape(E, BLOCK, 128).astype(BF16)
-
-    for s in range(2):
-        for k in range(4):
-            ty32[s, pl.ds(k, 4 * E, stride=4), :] = trows32[
-                pl.ds((12 if s == 0 else 0) + k, 4 * E, stride=16), :
-            ]
-    ty[...] = ty32[...].reshape(2, EX, EY, 16, 128).astype(BF16)
-    start(tent_copy)
-
-    loads[2].wait()
     grouped = jnp.concatenate(
         [
             jnp.concatenate(
@@ -303,7 +288,7 @@
         axis=0,
     )
     couple = jnp.dot(grouped, order[...], preferred_element_type=F32)
-    loads[3].wait()
+    loads[2].wait()
     for c in range(E):
         own = blocks_in[:, 128 * c : 128 * (c + 1)].astype(F32)
         side = couple[E * (c // 4) : E * (c // 4 + 1), 128 * (c % 4) : 128 * (c % 4 + 1)]
@@ -355,11 +340,28 @@
         x = jnp.dot(m_ref[e], stacked, preferred_element_type=F32)
         xb[BLOCK * e : BLOCK * (e + 1)] = x.astype(BF16)
 
-    loads[4].wait()
+    loads[3].wait()
     rhs = by_element(rhs_in, rhs_ref)
     residue = rhs - operate(0, guess)
     update = inverse * residue / centre
     send_traces(1, update)
+
+    loads[4].wait()
+    for c in range(E):
+        even = tent_in[:, 128 * c : 128 * (c + 1)].astype(F32)
+        odd = turn(even)
+        trows32[pl.ds(2 * c, E, stride=BLOCK), :] = jnp.where(left, even, odd)
+        trows32[pl.ds(2 * c + 1, E, stride=BLOCK), :] = jnp.where(left, odd, even)
+    t_ref[...] = trows32[...].reshape(E, BLOCK, 128).astype(BF16)
+
+    for s in range(2):
+        for k in range(4):
+            ty32[s, pl.ds(k, 4 * E, stride=4), :] = trows32[
+                pl.ds((12 if s == 0 else 0) + k, 4 * E, stride=16), :
+            ]
+    ty[...] = ty32[...].reshape(2, EX, EY, 16, 128).astype(BF16)
+    start(tent_copy)
+
     answer = guess + update
     factor = 1.0 / spread
 

time: 18.1 us -> 18.1 us (level)
  no operation moved by 1% of the time
where the time goes in v6:
time: 18.1 us; the launch traced here: 17.9 us
  Pallas kernels  17.2 us (95%)
  between operations  0.64 us (4%)
    pallas_call x1, Pallas kernels, on_device(): pl.pallas_call(lambda *refs: kernel(nx, ny, *refs), out_shape=shapes, in_...  15.1 us
    pallas_call x1, Pallas kernels, on_device(): pl.pallas_call(store_kernel, out_shape=shapes, in_specs=[hbm] * 3, out_sp...  2.13 us

profile of v6, /device:TPU:0, one launch (start us, length us, event | category | flops | bytes accessed | tf_op | source)
XLA Modules:
  0.0 17.9 jit_solution(15190391641324907846)
XLA Ops:
  0.6 15.1 %galerkin_smooth.1 = (f32[6,32,64]{2,1,0:T(8,128)}, f32[256,256]{1,0:T(8,128)}, f32[4,256,256]{2,1,0:T(8,128)}) custom-call(f32[2]{0:T(128)} %refs_0_.1, s32[32]{0:T(128)} %bitcast.21, s32[24]{0:T(128)} %bitcast.22, bf16[32,4096]{1,0:T(8,128)(2,1)} %bitcast.16, bf16[32,4096]{1,0:T(8,128)(2,1)} %bitcast.17, bf16[32,4096]{1,0:T(8,128)(2,1)} %bitcast.18, ...), custom_call_target="tpu_custom_call" | custom-call | tf_op jit(solution)/shard_map/galerkin_smooth/pallas_call | solution.py:497
  15.8 2.1 %store_results.1 = (f32[6,32,64]{2,1,0:T(8,128)}, f32[256,256]{1,0:T(8,128)}, f32[4,256,256]{2,1,0:T(8,128)}) custom-call(f32[6,32,64]{2,1,0:T(8,128)} %get-tuple-element.9.smoothed, f32[256,256]{1,0:T(8,128)} %get-tuple-element.10.local, f32[4,256,256]{2,1,0:T(8,128)} %get-tuple-element.11.ghost), custom_call_target="tpu_custom_call" | custom-call | tf_op jit(solution)/shard_map/store_results/pallas_call | solution.py:552
